TPU v7x, 512 devices: a whole 4x4x16 slice. The times are simulated.
512 devices in a mesh: ctx: 64 (over z, x_hi, core), tp: 8 (over x_lo, y).
Axes of the slice: x: 4 (x_hi: 2, x_lo: 2; x = x_hi * 2 + x_lo), y: 4, z: 16, core: 2. Of those that a mesh axis runs over, the one named last changes fastest.
Arguments:
- queries: bfloat16 [16384, 3072], P('ctx', 'tp'), may hold values from -64 to 64
- keys: bfloat16 [16384, 1024], P('ctx', 'tp'), may hold values from -12 to 12
- values: bfloat16 [16384, 1024], P('ctx', 'tp'), may hold values from -6 to 6
- out_weight: bfloat16 [3072, 5120], P('tp'), may hold values from -0.4375 to 0.4375
Outputs:
- attn_output: bfloat16 [16384, 5120], P('ctx', 'tp')
All inputs are finite; a program needn't handle non-finite values.
Results may differ from a plain program's by a relative error of at most 0.02.
Values may be sent and summed in bfloat16 or wider, within the bound.
No kernel may reach another device: no remote copies, remote signals or barrier semaphores. Data moves between devices by JAX's collectives and lax.ppermute only.
A program may use at most 64 MiB of HBM per device.

v0:
```python
import jax
import jax.numpy as jnp
from jax import lax
from jax.sharding import PartitionSpec as P

HEAD_DIM = 128
SPAN = 256
WINDOW = 128
INTER_POS = 511


rope_base = 10000000.0
masked_floor = -1e30


def shifted(block, axis, distance):
    devices = range(lax.axis_size(axis))
    route = [(i - distance, i) for i in devices if i - distance in devices]
    return lax.ppermute(block, axis, route)


def rope_tables(positions, head_dim):
    half_dim = head_dim // 2
    inverse_freq = rope_base ** (-(jnp.arange(half_dim, dtype=jnp.float32) * 2.0) / head_dim)
    angles = positions.astype(jnp.float32)[:, None] * inverse_freq[None, :]
    angles = jnp.concatenate([angles, angles], axis=1)
    return (jnp.cos(angles), jnp.sin(angles))


def rotate(vectors, cosine_table, sine_table):
    half_dim = vectors.shape[-1] // 2
    turned = jnp.concatenate([-vectors[..., half_dim:], vectors[..., :half_dim]], axis=-1)
    spread_shape = (cosine_table.shape[0],) + (1,) * (vectors.ndim - 2) + (cosine_table.shape[1],)
    return vectors * cosine_table.reshape(spread_shape) + turned * sine_table.reshape(spread_shape)


def query_positions(offset_in_span):
    successive = jnp.where(offset_in_span < WINDOW, SPAN + offset_in_span, INTER_POS)
    inter = jnp.zeros_like(offset_in_span) + INTER_POS
    return (offset_in_span, successive, inter)


def absorb(running, queries_rot, keys_part, values_part, allowed):
    highest, weight_sum, summed = running
    key_heads = keys_part.reshape(keys_part.shape[0], -1, HEAD_DIM)
    value_heads = values_part.reshape(values_part.shape[0], -1, HEAD_DIM)
    scores = jnp.einsum(
        "tkgd,jkd->kgtj", queries_rot, key_heads, preferred_element_type=jnp.float32
    )
    scores = jnp.where(allowed[None, None], scores * (1.0 / HEAD_DIM**0.5), masked_floor)
    highest_new = jnp.maximum(highest, jnp.max(scores, axis=-1))
    weights = jnp.where(allowed[None, None], jnp.exp(scores - highest_new[..., None]), 0.0)
    rescale = jnp.exp(highest - highest_new)
    weight_sum = weight_sum * rescale + jnp.sum(weights, axis=-1)
    summed = summed * rescale[..., None] + jnp.einsum(
        "kgtj,jkd->kgtd",
        weights.astype(jnp.bfloat16),
        value_heads,
        preferred_element_type=jnp.float32,
    )
    return (highest_new, weight_sum, summed)


def absorb_rows(running, queries_rot, keys_part, values_part, key_start, query_span):
    row_count = keys_part.shape[0]
    block_rows = 1024
    last_span = jnp.max(query_span)

    def piece_work(state, block_keys, block_values, block_start):
        key_rows = block_start + jnp.arange(block_keys.shape[0], dtype=jnp.int32)
        allowed = (key_rows >= 0)[None, :] & (
            (key_rows // SPAN)[None, :] <= query_span[:, None] - 2
        )
        useful = block_start // SPAN <= last_span - 2
        return lax.cond(
            useful,
            lambda inner_state: absorb(inner_state, queries_rot, block_keys, block_values, allowed),
            lambda inner_state: inner_state,
            state,
        )

    blocks = row_count // block_rows
    keys_blocks = keys_part.reshape(blocks, block_rows, keys_part.shape[1])
    values_blocks = values_part.reshape(blocks, block_rows, values_part.shape[1])

    def scan_block(state, element):
        block_keys, block_values, block_index = element
        return (
            piece_work(state, block_keys, block_values, key_start + block_index * block_rows),
            None,
        )

    running, _ = lax.scan(
        scan_block, running, (keys_blocks, values_blocks, jnp.arange(blocks, dtype=jnp.int32))
    )
    return running


def local(queries, keys, values, out_weight):
    local_count = queries.shape[0]
    heads_local = keys.shape[1] // HEAD_DIM
    group_size = queries.shape[1] // keys.shape[1]
    device = lax.axis_index("ctx")
    local_rows = jnp.arange(local_count, dtype=jnp.int32)
    offset_in_span = local_rows % SPAN
    query_span = (device * local_count + local_rows) // SPAN
    key_cosine, key_sine = rope_tables(offset_in_span, HEAD_DIM)
    keys_rot = rotate(
        keys.astype(jnp.float32).reshape(local_count, heads_local, HEAD_DIM), key_cosine, key_sine
    )
    keys_rot = keys_rot.astype(jnp.bfloat16).reshape(local_count, heads_local * HEAD_DIM)
    grouped = queries.astype(jnp.float32).reshape(local_count, heads_local, group_size, HEAD_DIM)
    rotated = []
    for position_table in query_positions(offset_in_span):
        cosine_table, sine_table = rope_tables(position_table, HEAD_DIM)
        rotated.append(rotate(grouped, cosine_table, sine_table).astype(jnp.bfloat16))
    state_shape = (heads_local, group_size, local_count)
    running = (
        jnp.full(state_shape, masked_floor, jnp.float32),
        jnp.zeros(state_shape, jnp.float32),
        jnp.zeros(state_shape + (HEAD_DIM,), jnp.float32),
    )
    local_span = local_rows // SPAN
    same_block = local_span[:, None] == local_span[None, :]
    running = absorb(
        running,
        rotated[0],
        keys_rot,
        values,
        same_block & (local_rows[:, None] >= local_rows[None, :]),
    )
    last_keys, last_values = shifted((keys_rot, values), "ctx", 1)
    previous_keys = jnp.concatenate([last_keys, keys_rot[: local_count - SPAN]], axis=0)
    previous_values = jnp.concatenate([last_values, values[: local_count - SPAN]], axis=0)
    running = absorb(
        running, rotated[1], previous_keys, previous_values, same_block & (query_span >= 1)[:, None]
    )
    running = absorb_rows(
        running,
        rotated[2],
        lax.all_gather(previous_keys, "ctx", axis=0, tiled=True),
        lax.all_gather(previous_values, "ctx", axis=0, tiled=True),
        jnp.int32(0) - SPAN,
        query_span,
    )
    highest, weight_sum, summed = running
    attended = (
        (summed / weight_sum[..., None])
        .transpose(2, 0, 1, 3)
        .reshape(local_count, heads_local * group_size * HEAD_DIM)
    )
    attended = attended.astype(jnp.bfloat16)
    partial_sum = jnp.dot(attended, out_weight, preferred_element_type=jnp.float32)
    return lax.psum_scatter(partial_sum.astype(jnp.bfloat16), "tp", scatter_dimension=1, tiled=True)


def solution(mesh):
    placed = (P("ctx", "tp"), P("ctx", "tp"), P("ctx", "tp"), P("tp", None))
    return jax.shard_map(
        local, mesh=mesh, in_specs=placed, out_specs=P("ctx", "tp"), check_vma=False
    )
```

profile of v0, /device:TPU:4, one launch (start us, length us, event | category | flops | bytes accessed | tf_op | source)
XLA Modules:
  0.0 483.8 jit_solution(13692821516681048529)
XLA Ops:
  6.6 0.9 convert_bitcast_fusion
  7.7 1.4 fusion.65
  9.1 1.9 collective-permute-start
  11.0 5.2 %collective-permute-done = bf16[256,128]{1,0:T(8,128)(2,1)S(1)} collective-permute-done((bf16[256,128]{1,0:T(8,128)(2,1)S(1)}, bf16[256,128]{1,0:T(8,128)(2,1)S(1)}, u32[]{:S(2)}, u32[]{:S(2)}) %collective-permute-start) | collective-permute-done | bytes 65568 | tf_op jit(solution)/shard_map/ppermute | solution.py:19
  16.2 0.6 copy-done
  16.9 1.9 collective-permute-start.1
  18.8 5.4 %collective-permute-done.1 = bf16[256,128]{1,0:T(8,128)(2,1)S(1)} collective-permute-done((bf16[256,128]{1,0:T(8,128)(2,1)}, bf16[256,128]{1,0:T(8,128)(2,1)S(1)}, u32[]{:S(2)}, u32[]{:S(2)}) %collective-permute-start.1) | collective-permute-done | bytes 65568 | tf_op jit(solution)/shard_map/ppermute | solution.py:19
  24.2 0.6 copy-done.2
  24.9 1.1 copy.23
  27.8 0.6 fusion.78
  31.2 139.4 %all-gather.3.cloned.1.call-done = bf16[16384,128]{1,0:T(8,128)(2,1)} async-done(((bf16[256,128]{1,0:T(8,128)(2,1)}), bf16[16384,128]{1,0:T(8,128)(2,1)}) %all-gather.3.cloned.1.call-update) | async-done | bytes 4194320 | tf_op jit(solution)/shard_map/all_gather | solution.py:141
  170.6 148.8 %all-gather.5.cloned.1.call-done = bf16[16384,128]{1,0:T(8,128)(2,1)} async-done(((bf16[256,128]{1,0:T(8,128)(2,1)}), bf16[16384,128]{1,0:T(8,128)(2,1)}) %all-gather.5.cloned.1.call-update) | async-done | bytes 4194320 | tf_op jit(solution)/shard_map/all_gather | solution.py:142
  319.4 27.1 %while.18 = (s32[]{:T(128)}, f32[1,3,256]{2,1,0:T(4,128)S(1)}, f32[1,3,256]{2,1,0:T(4,128)S(1)}, f32[1,3,256,128]{3,2,1,0:T(8,128)S(1)}, s32[16]{0:T(128)S(1)}, ...) while((s32[]{:T(128)}, f32[1,3,256]{2,1,0:T(4,128)S(1)}, ...), condition=%wide.region_10.11_spmd.clone, body=%wide.region_5.10_spmd.clone.sunk | while | flops 413624352 | bytes 12079197 | solution.py:93
  320.7 5.2 %conditional.3 = ((f32[1,3,256]{2,1,0:T(4,128)S(1)}, f32[1,3,256]{2,1,0:T(4,128)S(1)}, f32[1,3,256,128]{3,2,1,0:T(8,128)S(1)})) conditional(s32[]{:T(128)} %convert_element_type.141, (f32[1,3,256]{2,1,0:T(4,128)S(1)}, f32[1,3,256]{2,1,0:T(4,128)S(1)}, f32[1,3,256,128]{3,2,1,0:T(8,128)S(1)}) %tuple.85, (s32[]{:T(128)}, s32[]{:T(128)}, ...), branch_computations={%region_6.6_spmd, %region_7.9_spmd.clone} | conditional | flops 413620736 | bytes 12070200 | solution.py:75
  321.2 1.7 fusion.2
  322.9 2.2 fusion.12
  325.0 0.8 fusion.4
  325.9 0.6 dynamic_slice.45
  327.3 0.6 dynamic_slice.45
  328.7 0.6 dynamic_slice.45
  346.7 3.7 convolution_convert_fusion
  350.4 2.6 copy.39
  353.0 122.4 %reduce-scatter.4.cloned.1.call-done = bf16[640,256]{1,0:T(8,128)(2,1)} async-done(((bf16[5120,256]{1,0:T(8,128)(2,1)}), bf16[640,256]{1,0:T(8,128)(2,1)}) %reduce-scatter.4.cloned.1.call-update) | async-done | bytes 327696
  475.4 1.9 copy.40
  (162 shorter events, 13.2 us)
Async XLA Ops:
  6.5 164.0 %all-gather.3.cloned.1.call-start = ((), (), s32[]{:S(2)}) async-start(), calls=%async_computation.1 | async-start | bytes 4259840 | tf_op jit(solution)/shard_map/all_gather | solution.py:141
  9.1 7.1 %collective-permute-start = (bf16[256,128]{1,0:T(8,128)(2,1)S(1)}, bf16[256,128]{1,0:T(8,128)(2,1)S(1)}, u32[]{:S(2)}, u32[]{:S(2)}) collective-permute-start(bf16[256,128]{1,0:T(8,128)(2,1)S(1)} %get-tuple-element.563), channel_id=1, source_target_pairs={{0,8},{8,16},{16,24},{24,32},{32,40},{40,48},{48,56},{56,64},{64,7... | collective-permute-start | bytes 196616 | tf_op jit(solution)/shard_map/ppermute | solution.py:19
  16.2 0.6 copy-start
  16.8 302.6 %all-gather.5.cloned.1.call-start = ((), (), s32[]{:S(2)}) async-start(), calls=%async_computation.2 | async-start | bytes 4259840 | tf_op jit(solution)/shard_map/all_gather | solution.py:142
  16.9 7.3 %collective-permute-start.1 = (bf16[256,128]{1,0:T(8,128)(2,1)}, bf16[256,128]{1,0:T(8,128)(2,1)S(1)}, u32[]{:S(2)}, u32[]{:S(2)}) collective-permute-start(bf16[256,128]{1,0:T(8,128)(2,1)} %param.10), channel_id=1, source_target_pairs={{0,8},{8,16},{16,24},{24,32},{32,40},{40,48},{48,56},{56,64},{64,7... | collective-permute-start | bytes 196616 | tf_op jit(solution)/shard_map/ppermute | solution.py:19
  24.2 0.6 copy-start.2
  24.8 450.5 %reduce-scatter.4.cloned.1.call-start = ((), (), s32[]{:S(2)}) async-start(), calls=%async_computation.3 | async-start | bytes 2949120
  27.6 2.1 copy-start.1
  29.1 1.2 copy-start.4
  29.2 1.5 copy-start.3
Sparse Core Ops, SparseCore 0:
  17.0 153.5 all-gather.2
  173.9 145.4 all-gather.4
  353.1 122.2 reduce-scatter.3
where the time goes:
time: 485 us; the launch traced here: 484 us
  waiting for transfers between devices  421 us (87%)
  local copies, waits for them, and re-layouts  17.1 us (4%)
  between operations  14 us (3%)
  loops' own time  12.1 us (2%)
  matrix products  8.84 us (2%)
  other arithmetic  6.64 us (1%)
    all_gather x1, waiting for transfers between devices, local(): lax.all_gather(previous_values, 'ctx', axis=0, tiled=True)  149 us
    all_gather x1, waiting for transfers between devices, local(): lax.all_gather(previous_keys, 'ctx', axis=0, tiled=True)  139 us
    unnamed x4, waiting for transfers between devices  122 us
    another operation x1, loops' own time, absorb_rows(): lax.scan(scan_block, running, (keys_blocks, values_blocks, jnp.arange(blo...  11.8 us
    ppermute x2, waiting for transfers between devices, shifted(): return lax.ppermute(block, axis, route)  10.5 us
  transfers between devices with their start and end apart: 5, of which 5 were waited for; matrix products, arithmetic and copies ran while one was open for 1% of the time, Pallas kernels for 0%

commit v1 on v0

v1 whole, which is shorter than its diff:
```python
import functools

import jax
import jax.numpy as jnp
import numpy as np
from jax import lax
from jax.experimental import pallas as pl
from jax.experimental.pallas import tpu as pltpu
from jax.sharding import PartitionSpec as P

HEAD_DIM = 128
SPAN = 256
WINDOW = 128
INTER_POS = 511
GROUP = 3
ROWS = GROUP * SPAN
ROPE_BASE = 10000000.0
FLOOR = -1e30
SCALE = float(np.log2(np.e) / np.sqrt(HEAD_DIM))
BF = jnp.bfloat16
F32 = jnp.float32
VMEM = pl.BlockSpec(memory_space=pltpu.VMEM)
SMEM = pl.BlockSpec(memory_space=pltpu.SMEM)
PART_ROWS = ROWS + 16 * GROUP

N_Z, N_ZH, N_ZL = 16, 4, 4
STEPS = (-1, 1, 2)
CTX = 64
TP = 8


def rope_tables():
    half = HEAD_DIM // 2
    freq = np.float32(ROPE_BASE) ** (-(np.arange(half, dtype=np.float32) * np.float32(2.0)) / np.float32(HEAD_DIM))
    freq = freq.astype(np.float32)

    def table(positions):
        angles = (positions.astype(np.float32)[:, None] * freq[None, :]).astype(np.float32)
        return np.concatenate([np.cos(angles), np.sin(angles)], axis=1).astype(np.float32)

    offset = np.arange(SPAN)
    succ = np.where(offset < WINDOW, SPAN + offset, INTER_POS)
    inter = np.full((8,), INTER_POS)
    return table(offset), table(succ), table(inter)


def full_tables(table):
    lane = lax.broadcasted_iota(jnp.int32, table.shape, 1)
    turned = pltpu.roll(table, HEAD_DIM // 2, 1)
    first = lane < HEAD_DIM // 2
    return jnp.where(first, table, turned), jnp.where(first, -turned, table)


def rotated(x, tables):
    return x * tables[0] + pltpu.roll(x, HEAD_DIM // 2, 1) * tables[1]


def prepare_kernel(queries, keys, values, own, succ, inter, kv, q_pair, q_intra):
    own_tables = full_tables(own[...])
    kv[:SPAN, :] = rotated(keys[...].astype(F32), own_tables).astype(BF)
    kv[SPAN:, :] = values[...]
    succ_tables = full_tables(succ[...])
    inter_tables = [jnp.broadcast_to(t[0:1, :], (SPAN, HEAD_DIM)) for t in full_tables(inter[...])]
    for h in range(GROUP):
        x = queries[:, h * HEAD_DIM:(h + 1) * HEAD_DIM].astype(F32)
        rows = slice(h * SPAN, (h + 1) * SPAN)
        q_pair[0, rows, :] = rotated(x, inter_tables).astype(BF)
        q_pair[1, rows, :] = rotated(x, succ_tables).astype(BF)
        q_intra[rows, :] = rotated(x, own_tables).astype(BF)


def prepare(*operands):
    def whole(x):
        return pl.BlockSpec(x.shape, lambda i: (0,) * len(x.shape))

    outs = (shape((2 * SPAN, HEAD_DIM), BF), shape((2, ROWS, HEAD_DIM), BF), shape((ROWS, HEAD_DIM), BF))
    return pl.pallas_call(
        prepare_kernel,
        grid=(1,),
        out_shape=outs,
        in_specs=[whole(x) for x in operands],
        out_specs=tuple(whole(x) for x in outs),
        compiler_params=pltpu.CompilerParams(vmem_limit_bytes=60 * 1024 * 1024),
        cost_estimate=pl.CostEstimate(flops=10 ** 6, bytes_accessed=2 ** 20, transcendentals=0),
    )(*operands)


def scores(q, k):
    return lax.dot_general(q, k, (((1,), (1,)), ((), ())), preferred_element_type=F32)


def absorb(state, q, k, v, mask=None):
    top, total, summed = state
    lanes = k.shape[0] // HEAD_DIM
    s = scores(q[...], k)
    if mask is not None:
        s = jnp.where(mask, s, FLOOR)
    peak = s[:, :HEAD_DIM]
    for i in range(1, lanes):
        peak = jnp.maximum(peak, s[:, i * HEAD_DIM:(i + 1) * HEAD_DIM])
    old = top[...]
    new = jnp.maximum(old, jnp.max(peak, axis=1, keepdims=True))
    base = new * SCALE
    fade = jnp.exp2(old * SCALE - base)
    parts = []
    mass = total[...] * fade
    for i in range(lanes):
        w = jnp.exp2(s[:, i * HEAD_DIM:(i + 1) * HEAD_DIM] * SCALE - base)
        if mask is not None:
            w = jnp.where(mask[:, i * HEAD_DIM:(i + 1) * HEAD_DIM], w, 0.0)
        mass = mass + w
        parts.append(w.astype(BF))
    w = jnp.concatenate(parts, axis=1)
    top[...] = new
    total[...] = mass
    summed[...] = summed[...] * fade + jnp.dot(w, v, preferred_element_type=F32)


def absorb_buffer(state, span, q_ref, buf, row, first, step):
    low = jnp.minimum(first, first + 3 * step)
    count = jnp.clip((span - 2 - low + 64) // 16 - 3, 0, 4)
    start = jnp.where(step > 0, 0, 4 - count)

    def block(j):
        return pl.multiple_of(row + j * (2 * SPAN), 2 * SPAN)

    for size in (4, 3):
        @pl.when(count == size)
        def _(size=size):
            k = jnp.concatenate([buf[pl.ds(block(start + j), SPAN), :] for j in range(size)], axis=0)
            v = jnp.concatenate(
                [buf[pl.ds(pl.multiple_of(block(start + j) + SPAN, SPAN), SPAN), :] for j in range(size)], axis=0)
            absorb(state, q_ref.at[0], k, v)

    def one(j, carry):
        distance = span - (first + step * j)

        @pl.when(jnp.logical_or(distance == 1, jnp.logical_and(distance >= 2, count < 3)))
        def _():
            kind = jnp.where(distance == 1, 1, 0)
            k = buf[pl.ds(block(j), SPAN), :]
            v = buf[pl.ds(pl.multiple_of(block(j) + SPAN, SPAN), SPAN), :]
            absorb(state, q_ref.at[kind], k, v)

        return carry

    lax.fori_loop(0, N_ZH, one, 0)


def spans_of(place, step, other):
    core = lax.rem(place, 2)
    which = 1 - core if other else core
    residue = lax.rem(place // 4 + step + N_Z, N_ZL)
    first = residue * 4 + lax.rem(place // 2, 2) * 2 + which
    return first + jnp.where(which == 1, 48, 0), jnp.where(which == 1, -16, 16)


def targets_of(place):
    return place, place + 2 - 4 * lax.rem(place // 2, 2)


def pick(values, i):
    result = values[-1]
    for j in range(len(values) - 2, -1, -1):
        result = jnp.where(i == j, values[j], result)
    return result


def absorb_all(targets, segments, q_of, buf, states):
    size = N_ZH * 2 * SPAN
    count = len(segments)

    def one(i, carry):
        target, segment = i // count, lax.rem(i, count)
        absorb_buffer(
            [x.at[target] for x in states], pick(targets, target), q_of(target), buf, segment * size,
            pick([first for first, _ in segments], segment), pick([step for _, step in segments], segment),
        )
        return carry

    lax.fori_loop(0, len(targets) * count, one, 0)


def copy_all(sources, target):
    at = 0
    for source in sources:
        target[at:at + source.shape[0]] = source[...]
        at += source.shape[0]


def first_kernel(place, q_own, q_peer, q_intra, kv, far, far_other, top, total, summed, done, q_all, joined):
    done[...] = jnp.zeros(done.shape, F32)
    states = (top, total, summed)
    top[...] = jnp.full(top.shape, FLOOR, F32)
    total[...] = jnp.zeros(total.shape, F32)
    summed[...] = jnp.zeros(summed.shape, F32)
    q_all[0] = q_own[...]
    q_all[1] = q_peer[...]
    copy_all([far, far_other], joined)
    row = lax.broadcasted_iota(jnp.int32, (ROWS, SPAN), 0) % SPAN
    column = lax.broadcasted_iota(jnp.int32, (ROWS, SPAN), 1)
    absorb([x.at[0] for x in states], q_intra, kv[:SPAN, :], kv[SPAN:, :], mask=row >= column)
    here = place[0]
    absorb_all(targets_of(here), [spans_of(here, 0, False), spans_of(here, 0, True)], lambda i: q_all.at[i], joined, states)


def near_kernel(steps, place, q_own, q_peer, before, *refs):
    bufs, ins, states = refs[:len(steps)], refs[len(steps):len(steps) + 3], refs[len(steps) + 3:len(steps) + 6]
    done, joined, q_all = refs[len(steps) + 6:]
    done[...] = before[...]
    for source, target in zip(ins, states):
        target[...] = source[...]
    q_all[0] = q_own[...]
    q_all[1] = q_peer[...]
    copy_all(bufs, joined)
    here = place[0]
    absorb_all(targets_of(here), [spans_of(here, step, False) for step in steps], lambda i: q_all.at[i], joined, states)


def three_terms(x):
    hi = x.astype(BF)
    rest = x - hi.astype(F32)
    mid = rest.astype(BF)
    low = (rest - mid.astype(F32)).astype(BF)
    return hi, mid, low


def last_segments(place):
    return [spans_of(place, step, True) for step in STEPS]


def peer_kernel(place, q_peer, two, three, *refs):
    ins, out, state, joined = refs[:3], refs[3], refs[4:7], refs[7]
    for source, target in zip(ins, state):
        target[0] = source[1]
    copy_all([two, three], joined)
    here = place[0]
    absorb_all(targets_of(here)[1:], last_segments(here), lambda i: q_peer, joined, state)
    state = [x.at[0] for x in state]
    lane = lax.broadcasted_iota(jnp.int32, (SPAN, HEAD_DIM), 1)
    for h in range(GROUP):
        rows = slice(h * SPAN, (h + 1) * SPAN)
        mass = jnp.sum(state[1][rows, :], axis=1, keepdims=True)
        safe = jnp.where(mass > 0.0, mass, 1.0)
        out[rows, :] = (state[2][rows, :] / safe).astype(BF)
        stats = jnp.zeros((SPAN, HEAD_DIM), F32)
        terms = three_terms(state[0][rows, :]) + three_terms(jnp.broadcast_to(mass, (SPAN, HEAD_DIM)))
        for i, term in enumerate(terms):
            stats = jnp.where(lane == i, term.astype(F32), stats)
        stats = stats.T
        both = jnp.concatenate([stats[:8, :HEAD_DIM], stats[:8, HEAD_DIM:]], axis=0)
        out[ROWS + 16 * h:ROWS + 16 * (h + 1), :] = both.astype(BF)


def own_kernel(place, q_own, two, three, *refs):
    ins, outs, joined = refs[:3], refs[3:6], refs[6]
    for source, target in zip(ins, outs):
        target[...] = source[0:1]
    copy_all([two, three], joined)
    here = place[0]
    absorb_all(targets_of(here)[:1], last_segments(here), lambda i: q_own, joined, outs)


def merge(top, total, summed, part, out):
    for h in range(GROUP):
        rows = slice(h * SPAN, (h + 1) * SPAN)
        both = part[ROWS + 16 * h:ROWS + 16 * (h + 1), :].astype(F32)
        stats = jnp.concatenate([both[:8, :], both[8:, :]], axis=1)
        stats = jnp.concatenate([stats, jnp.zeros((HEAD_DIM - 8, SPAN), F32)], axis=0).T
        other_top = stats[:, 0:1] + stats[:, 1:2] + stats[:, 2:3]
        other_mass = stats[:, 3:4] + stats[:, 4:5] + stats[:, 5:6]
        own_top = top[rows, :][:, 0:1]
        own_mass = jnp.sum(total[rows, :], axis=1, keepdims=True)
        peak = jnp.maximum(own_top, other_top)
        own_scale = jnp.exp2((own_top - peak) * SCALE)
        other_scale = jnp.exp2((other_top - peak) * SCALE) * other_mass
        norm = 1.0 / (own_mass * own_scale + other_scale)
        value = summed[rows, :] * (own_scale * norm) + part[rows, :].astype(F32) * (other_scale * norm)
        out[:, h * HEAD_DIM:(h + 1) * HEAD_DIM] = value.astype(BF)


def project_kernel(top, total, summed, part, weight, out, attended):
    @pl.when(pl.program_id(0) == 0)
    def _():
        merge(top.at[0], total.at[0], summed.at[0], part, attended)

    out[0] = jnp.dot(attended[...], weight[...], preferred_element_type=F32).astype(BF)


def project(state, part, weight):
    depth, width = weight.shape[0], weight.shape[1] // TP
    whole = pl.BlockSpec((1, ROWS, HEAD_DIM), lambda t: (0, 0, 0))
    return pl.pallas_call(
        project_kernel,
        grid=(TP,),
        out_shape=shape((TP, SPAN, width), BF),
        in_specs=[whole] * 3 + [
            pl.BlockSpec((PART_ROWS, HEAD_DIM), lambda t: (0, 0)), pl.BlockSpec((depth, width), lambda t: (0, t))
        ],
        out_specs=pl.BlockSpec((1, SPAN, width), lambda t: (t, 0, 0)),
        scratch_shapes=[pltpu.VMEM((SPAN, depth), BF)],
        compiler_params=pltpu.CompilerParams(vmem_limit_bytes=16 * 1024 * 1024),
        cost_estimate=pl.CostEstimate(
            flops=2 * SPAN * depth * TP * width, bytes_accessed=2 * TP * width * (depth + SPAN), transcendentals=0),
    )(*state, part, weight)


def sum_kernel(parts, out):
    total = parts[0].astype(F32)
    for t in range(1, TP):
        total = total + parts[t].astype(F32)
    out[...] = total.astype(BF)


def sum_parts(parts):
    _, rows, width = parts.shape
    block = rows // 4
    return pl.pallas_call(
        sum_kernel,
        grid=(4,),
        out_shape=shape((rows, width), BF),
        in_specs=[pl.BlockSpec((TP, block, width), lambda t: (0, t, 0))],
        out_specs=pl.BlockSpec((block, width), lambda t: (t, 0)),
        compiler_params=pltpu.CompilerParams(vmem_limit_bytes=12 * 1024 * 1024),
        cost_estimate=pl.CostEstimate(flops=TP * rows * width, bytes_accessed=2 * TP * rows * width, transcendentals=0),
    )(parts)


def call(kernel, outs, operands, flops, scratch=(), smem_first=True):
    specs = [VMEM] * len(operands)
    if smem_first:
        specs[0] = SMEM
    nbytes = sum(int(np.prod(x.shape)) * x.dtype.itemsize for x in list(operands) + list(outs))
    result = pl.pallas_call(
        kernel,
        out_shape=tuple(outs),
        in_specs=specs,
        out_specs=tuple([VMEM] * len(outs)),
        scratch_shapes=list(scratch),
        compiler_params=pltpu.CompilerParams(vmem_limit_bytes=18 * 1024 * 1024),
        cost_estimate=pl.CostEstimate(flops=flops, bytes_accessed=nbytes, transcendentals=0),
    )(*operands)
    return result


def shape(dims, dtype):
    return jax.ShapeDtypeStruct(dims, dtype)


def z_route(core0, core1):
    route = []
    for z in range(N_Z):
        for r in range(4):
            d = core1 if r % 2 else core0
            route.append((z * 4 + r, ((z + d) % N_Z) * 4 + r))
    return route


SWAP_CORE = [(i, i ^ 1) for i in range(CTX)]
SWAP_HI = [(i, i ^ 2) for i in range(CTX)]
FAR_GROUPS = [
    [a * 16 + r for a in (range(N_ZH) if r % 2 == 0 else reversed(range(N_ZH)))] for r in range(16)
]


def local(queries, keys, values, out_weight):
    own_table, succ_table, inter_table = (jnp.asarray(t) for t in rope_tables())
    place = lax.axis_index("ctx").astype(jnp.int32).reshape(1)

    kv, q_own, q_intra = prepare(queries, keys, values, own_table, succ_table, inter_table)
    q_peer = lax.ppermute(q_own, "ctx", SWAP_HI)
    far = lax.all_gather(kv, "ctx", axis=0, tiled=True, axis_index_groups=FAR_GROUPS)
    far, q_peer = lax.optimization_barrier((far, q_peer))
    near = [
        lax.ppermute(far, "ctx", z_route(1, 1)),
        lax.ppermute(far, "ctx", z_route(-1, -1)),
        lax.ppermute(far, "ctx", z_route(2, -2)),
    ]
    far_other = lax.ppermute(far, "ctx", SWAP_CORE)

    state_shapes = [shape((1, ROWS, HEAD_DIM), F32)] * 3
    both_shapes = [shape((2, ROWS, HEAD_DIM), F32)] * 3
    token = shape((8, HEAD_DIM), F32)
    tile = 4 * ROWS * SPAN * HEAD_DIM
    size = far.shape[0]
    q_scratch = pltpu.VMEM((2, 2, ROWS, HEAD_DIM), BF)

    *state, done = call(
        first_kernel, both_shapes + [token], [place, q_own, q_peer, q_intra, kv, far, far_other], 17 * tile,
        scratch=[q_scratch, pltpu.VMEM((2 * size, HEAD_DIM), BF)],
    )
    *near[:2], done = lax.optimization_barrier((*near[:2], done))
    *state, done, joined = call(
        functools.partial(near_kernel, STEPS[:2]), both_shapes + [token, shape((2 * size, HEAD_DIM), BF)],
        [place, q_own, q_peer, done] + near[:2] + state, 16 * tile, scratch=[q_scratch],
    )
    two = lax.ppermute(joined, "ctx", SWAP_CORE)
    near[2], done = lax.optimization_barrier((near[2], done))
    three = lax.ppermute(near[2], "ctx", SWAP_CORE)
    *state, _, _ = call(
        functools.partial(near_kernel, STEPS[2:]), both_shapes + [token, shape((size, HEAD_DIM), BF)],
        [place, q_own, q_peer, done] + near[2:] + state, 8 * tile, scratch=[q_scratch],
    )
    last_scratch = pltpu.VMEM((3 * size, HEAD_DIM), BF)
    (part,) = call(
        peer_kernel, [shape((PART_ROWS, HEAD_DIM), BF)], [place, q_peer, two, three] + state, 12 * tile,
        scratch=[pltpu.VMEM((1, ROWS, HEAD_DIM), F32)] * 3 + [last_scratch],
    )
    part_here = lax.ppermute(part, "ctx", SWAP_HI)
    own = call(own_kernel, state_shapes, [place, q_own, two, three] + state, 12 * tile, scratch=[last_scratch])
    partial = project(own, part_here, out_weight)
    return sum_parts(lax.all_to_all(partial, "tp", 0, 0))


def solution(mesh):
    placed = (P("ctx", "tp"), P("ctx", "tp"), P("ctx", "tp"), P("tp", None))
    return jax.shard_map(
        local, mesh=mesh, in_specs=placed, out_specs=P("ctx", "tp"), check_vma=False
    )
```

time: 485 us -> 133 us (0.27)
  the two profiles are of different devices: /device:TPU:4 before, /device:TPU:32 now
where the time goes in v1:
time: 133 us
  blocking collectives  69.2 us (52%)
  starting transfers between devices  23.6 us (18%)
  waiting for transfers between devices  21.1 us (16%)
  Pallas kernels  15.8 us (12%)
  local copies, waits for them, and re-layouts  2.83 us (2%)
    all_to_all x1, blocking collectives, local(): return sum_parts(lax.all_to_all(partial, 'tp', 0, 0))  36.3 us
    all_gather x1, blocking collectives, local(): lax.all_gather(kv, 'ctx', axis=0, tiled=True, axis_index_groups=FAR_GROUPS)  32.9 us
    ppermute x1, waiting for transfers between devices, local(): lax.ppermute(far, 'ctx', z_route(2, -2))  9.93 us
    pallas_call x5, Pallas kernels, call(): pl.pallas_call(kernel, out_shape=tuple(outs), in_specs=specs, out_specs=t...  7.6 us
    ppermute x1, waiting for transfers between devices, local(): part_here = lax.ppermute(part, 'ctx', SWAP_HI)  7.15 us
    ppermute x1, starting transfers between devices, local(): q_peer = lax.ppermute(q_own, 'ctx', SWAP_HI)  4.92 us
    ppermute x1, starting transfers between devices, local(): lax.ppermute(far, 'ctx', z_route(2, -2))  4.26 us
    pallas_call x1, Pallas kernels, project(): pl.pallas_call(project_kernel, grid=(TP,), out_shape=shape((TP, SPAN, wid...  4.24 us
  transfers between devices with their start and end apart: 8, of which 5 were waited for; matrix products, arithmetic and copies ran while one was open for 0% of the time, Pallas kernels for 5%

profile of v1, /device:TPU:32, one launch (start us, length us, event | category | flops | bytes accessed | tf_op | source)
XLA Modules:
  0.0 132.7 jit_solution(12923551759570505881)
XLA Ops:
  0.0 2.2 %shard_map.73 = (bf16[512,128]{1,0:T(8,128)(2,1)}, bf16[2,768,128]{2,1,0:T(8,128)(2,1)}, bf16[768,128]{1,0:T(8,128)(2,1)}) custom-call(bf16[256,384]{1,0:T(8,128)(2,1)} %queries.1, bf16[256,128]{1,0:T(8,128)(2,1)} %keys.1, bf16[256,128]{1,0:T(8,128)(2,1)} %values.1, f32[256,128]{1,0:T(8,128)} %constant.12.clone.own, f32[256,128]{1,0:T(8,128)} %constant.13.clone.succ, ...), custom_call_target="tpu_custom_call" | custom-call | flops 1000000 | bytes 1048576 | tf_op jit(solution)/shard_map/pallas_call | solution.py:77
  2.3 4.9 %collective-permute-start = (bf16[2,768,128]{2,1,0:T(8,128)(2,1)}, bf16[2,768,128]{2,1,0:T(8,128)(2,1)S(1)}, u32[]{:S(2)}, u32[]{:S(2)}) collective-permute-start(bf16[2,768,128]{2,1,0:T(8,128)(2,1)} %get-tuple-element.30.q_own), channel_id=1, source_target_pairs={{0,16},{8,24},{16,0},{24,8},{32,48},{40,56},{48,32},{56,40},{64,80... | collective-permute-start | bytes 1179656 | tf_op jit(solution)/shard_map/ppermute | solution.py:371
  7.2 32.9 %all_gather.3.far = bf16[2048,128]{1,0:T(8,128)(2,1)S(1)} all-gather(bf16[512,128]{1,0:T(8,128)(2,1)} %get-tuple-element.31.kv), channel_id=1, replica_groups={{0,128,256,384},{392,264,136,8},{16,144,272,400},{408,280,152,24},{32,1..., dimensions={0}, use_global_device_ids=true | all-gather | bytes 655360 | tf_op jit(solution)/shard_map/all_gather | solution.py:372
  40.1 1.9 %collective-permute-start.3 = (bf16[2048,128]{1,0:T(8,128)(2,1)S(1)}, bf16[2048,128]{1,0:T(8,128)(2,1)S(1)}, u32[]{:S(2)}, u32[]{:S(2)}) collective-permute-start(bf16[2048,128]{1,0:T(8,128)(2,1)S(1)} %all_gather.3.far), channel_id=1, source_target_pairs={{0,8},{8,0},{16,24},{24,16},{32,40},{40,32},{48,56},{56,48},{64,72... | collective-permute-start | bytes 1572872 | tf_op jit(solution)/shard_map/ppermute | solution.py:379
  42.0 1.9 %collective-permute-start.2 = (bf16[2048,128]{1,0:T(8,128)(2,1)S(1)}, bf16[2048,128]{1,0:T(8,128)(2,1)S(1)}, u32[]{:S(2)}, u32[]{:S(2)}) collective-permute-start(bf16[2048,128]{1,0:T(8,128)(2,1)S(1)} %all_gather.3.far), channel_id=1, source_target_pairs={{0,480},{8,488},{16,496},{24,504},{32,0},{40,8},{48,16},{56,24},{6... | collective-permute-start | bytes 1572872 | tf_op jit(solution)/shard_map/ppermute | solution.py:376
  44.0 3.9 %collective-permute-start.1 = (bf16[2048,128]{1,0:T(8,128)(2,1)S(1)}, bf16[2048,128]{1,0:T(8,128)(2,1)S(1)}, u32[]{:S(2)}, u32[]{:S(2)}) collective-permute-start(bf16[2048,128]{1,0:T(8,128)(2,1)S(1)} %all_gather.3.far), channel_id=1, source_target_pairs={{0,32},{8,40},{16,48},{24,56},{32,64},{40,72},{48,80},{56,88},{64,... | collective-permute-start | bytes 1572872 | tf_op jit(solution)/shard_map/ppermute | solution.py:375
  47.9 4.3 %collective-permute-start.5 = (bf16[2048,128]{1,0:T(8,128)(2,1)S(1)}, bf16[2048,128]{1,0:T(8,128)(2,1)S(1)}, u32[]{:S(2)}, u32[]{:S(2)}) collective-permute-start(bf16[2048,128]{1,0:T(8,128)(2,1)S(1)} %all_gather.3.far), channel_id=1, source_target_pairs={{0,64},{8,456},{16,80},{24,472},{32,96},{40,488},{48,112},{56,504}... | collective-permute-start | bytes 1572872 | tf_op jit(solution)/shard_map/ppermute | solution.py:377
  52.2 1.0 copy-done.1
  54.1 0.9 copy-done.4
  55.0 2.2 %shard_map.74 = (f32[2,768,128]{2,1,0:T(8,128)S(1)}, f32[2,768,128]{2,1,0:T(8,128)S(1)}, f32[2,768,128]{2,1,0:T(8,128)S(1)}, f32[8,128]{1,0:T(8,128)S(1)}) custom-call(s32[1]{0:T(128)} %bitcast.place, bf16[2,768,128]{2,1,0:T(8,128)(2,1)S(1)} %copy-done.1, bf16[2,768,128]{2,1,0:T(8,128)(2,1)S(1)} %collective-permute-done.q_peer, ...), custom_call_target="tpu_custom_call" | custom-call | flops 1711276032 | bytes 4526084 | tf_op jit(solution)/shard_map/pallas_call | solution.py:334
  57.2 1.7 %collective-permute-done.2.refs_1_ = bf16[2048,128]{1,0:T(8,128)(2,1)S(1)} collective-permute-done((bf16[2048,128]{1,0:T(8,128)(2,1)S(1)}, bf16[2048,128]{1,0:T(8,128)(2,1)S(1)}, u32[]{:S(2)}, u32[]{:S(2)}) %collective-permute-start.2) | collective-permute-done | bytes 524320 | tf_op jit(solution)/shard_map/ppermute | solution.py:376
  58.9 1.8 %collective-permute-done.1.refs_0_ = bf16[2048,128]{1,0:T(8,128)(2,1)S(1)} collective-permute-done((bf16[2048,128]{1,0:T(8,128)(2,1)S(1)}, bf16[2048,128]{1,0:T(8,128)(2,1)S(1)}, u32[]{:S(2)}, u32[]{:S(2)}) %collective-permute-start.1) | collective-permute-done | bytes 524320 | tf_op jit(solution)/shard_map/ppermute | solution.py:375
  60.7 1.8 %shard_map.75 = (f32[2,768,128]{2,1,0:T(8,128)S(1)}, f32[2,768,128]{2,1,0:T(8,128)S(1)}, f32[2,768,128]{2,1,0:T(8,128)S(1)}, f32[8,128]{1,0:T(8,128)S(1)}, bf16[4096,128]{1,0:T(8,128)(2,1)S(1)}) custom-call(s32[1]{0:T(128)} %bitcast.place, bf16[2,768,128]{2,1,0:T(8,128)(2,1)S(1)} %copy-done.2, bf16[2,768,128]{2,1,0:T(8,128)(2,1)S(1)} %collective-permute-done.q_peer, ...), custom_call_target="tpu_custom_call" | custom-call | flops 1610612736 | bytes 7610372 | tf_op jit(solution)/shard_map/pallas_call | solution.py:334
  62.5 1.9 %collective-permute-start.4 = (bf16[4096,128]{1,0:T(8,128)(2,1)S(1)}, bf16[4096,128]{1,0:T(8,128)(2,1)S(1)}, u32[]{:S(2)}, u32[]{:S(2)}) collective-permute-start(bf16[4096,128]{1,0:T(8,128)(2,1)S(1)} %get-tuple-element.42), channel_id=1, source_target_pairs={{0,8},{8,0},{16,24},{24,16},{32,40},{40,32},{48,56},{56,48},{64,72... | collective-permute-start | bytes 3145736 | tf_op jit(solution)/shard_map/ppermute | solution.py:397
  64.4 9.9 %collective-permute-done.5.refs_0_ = bf16[2048,128]{1,0:T(8,128)(2,1)S(1)} collective-permute-done((bf16[2048,128]{1,0:T(8,128)(2,1)S(1)}, bf16[2048,128]{1,0:T(8,128)(2,1)S(1)}, u32[]{:S(2)}, u32[]{:S(2)}) %collective-permute-start.5) | collective-permute-done | bytes 524320 | tf_op jit(solution)/shard_map/ppermute | solution.py:377
  74.4 2.1 %collective-permute-start.6 = (bf16[2048,128]{1,0:T(8,128)(2,1)S(1)}, bf16[2048,128]{1,0:T(8,128)(2,1)S(1)}, u32[]{:S(2)}, u32[]{:S(2)}) collective-permute-start(bf16[2048,128]{1,0:T(8,128)(2,1)S(1)} %collective-permute-done.5.refs_0_), channel_id=1, source_target_pairs={{0,8},{8,0},{16,24},{24,16},{32,40},{40,32},{48,56},{56,48},{64,72... | collective-permute-start | bytes 1572872 | tf_op jit(solution)/shard_map/ppermute | solution.py:399
  76.5 1.2 shard_map.76
  78.2 1.4 %shard_map.78 = bf16[816,128]{1,0:T(8,128)(2,1)S(1)} custom-call(s32[1]{0:T(128)} %bitcast.place, bf16[2,768,128]{2,1,0:T(8,128)(2,1)S(1)} %collective-permute-done.q_peer, bf16[4096,128]{1,0:T(8,128)(2,1)S(1)} %collective-permute-done.4.two, bf16[2048,128]{1,0:T(8,128)(2,1)S(1)} %collective-permute-done.6.three, ...), custom_call_target="tpu_custom_call" | custom-call | flops 1207959552 | bytes 4534276 | tf_op jit(solution)/shard_map/pallas_call | solution.py:334
  79.6 2.7 %collective-permute-start.7 = (bf16[816,128]{1,0:T(8,128)(2,1)S(1)}, bf16[816,128]{1,0:T(8,128)(2,1)S(1)}, u32[]{:S(2)}, u32[]{:S(2)}) collective-permute-start(bf16[816,128]{1,0:T(8,128)(2,1)S(1)} %shard_map.78), channel_id=1, source_target_pairs={{0,16},{8,24},{16,0},{24,8},{32,48},{40,56},{48,32},{56,40},{64,80... | collective-permute-start | bytes 626696 | tf_op jit(solution)/shard_map/ppermute | solution.py:409
  82.3 1.0 shard_map.77
  83.3 7.1 %collective-permute-done.7.part = bf16[816,128]{1,0:T(8,128)(2,1)S(1)} collective-permute-done((bf16[816,128]{1,0:T(8,128)(2,1)S(1)}, bf16[816,128]{1,0:T(8,128)(2,1)S(1)}, u32[]{:S(2)}, u32[]{:S(2)}) %collective-permute-start.7) | collective-permute-done | bytes 208928 | tf_op jit(solution)/shard_map/ppermute | solution.py:409
  90.4 4.2 %shard_map.79 = bf16[8,256,640]{2,1,0:T(8,128)(2,1)S(1)} custom-call(f32[1,768,128]{2,1,0:T(8,128)S(1)} %get-tuple-element.52.top, f32[1,768,128]{2,1,0:T(8,128)S(1)} %get-tuple-element.53.total, f32[1,768,128]{2,1,0:T(8,128)S(1)} %get-tuple-element.54.summed, bf16[816,128]{1,0:T(8,128)(2,1)S(1)} %collective-permute-done.7.part, bf16[384,5120]{1,0:T(8,128)(2,1)S(1)} %copy-done), custom_call_target="tpu_custom_call" | custom-call | flops 1006632960 | bytes 6553600 | tf_op jit(solution)/shard_map/pallas_call | solution.py:293
  94.7 36.3 %all_to_all.5.parts = bf16[8,256,640]{2,1,0:T(8,128)(2,1)S(1)} all-to-all(bf16[8,256,640]{2,1,0:T(8,128)(2,1)S(1)} %shard_map.79), channel_id=1, replica_groups=mesh['ctx'=64,'tp'=8] {'tp'}, dimensions={0} | all-to-all | bytes 5242880 | tf_op jit(solution)/shard_map/all_to_all | solution.py:412
  130.9 1.7 %shard_map.80 = bf16[256,640]{1,0:T(8,128)(2,1)} custom-call(bf16[8,256,640]{2,1,0:T(8,128)(2,1)S(1)} %all_to_all.5.parts), custom_call_target="tpu_custom_call" | custom-call | flops 1310720 | bytes 2621440 | tf_op jit(solution)/shard_map/pallas_call | solution.py:318
  (12 shorter events, 1.4 us)
Async XLA Ops:
  2.3 37.9 %collective-permute-start = (bf16[2,768,128]{2,1,0:T(8,128)(2,1)}, bf16[2,768,128]{2,1,0:T(8,128)(2,1)S(1)}, u32[]{:S(2)}, u32[]{:S(2)}) collective-permute-start(bf16[2,768,128]{2,1,0:T(8,128)(2,1)} %get-tuple-element.30.q_own), channel_id=1, source_target_pairs={{0,16},{8,24},{16,0},{24,8},{32,48},{40,56},{48,32},{56,40},{64,80... | collective-permute-start | bytes 1179656 | tf_op jit(solution)/shard_map/ppermute | solution.py:371
  40.1 12.1 %collective-permute-start.3 = (bf16[2048,128]{1,0:T(8,128)(2,1)S(1)}, bf16[2048,128]{1,0:T(8,128)(2,1)S(1)}, u32[]{:S(2)}, u32[]{:S(2)}) collective-permute-start(bf16[2048,128]{1,0:T(8,128)(2,1)S(1)} %all_gather.3.far), channel_id=1, source_target_pairs={{0,8},{8,0},{16,24},{24,16},{32,40},{40,32},{48,56},{56,48},{64,72... | collective-permute-start | bytes 1572872 | tf_op jit(solution)/shard_map/ppermute | solution.py:379
  42.0 16.9 %collective-permute-start.2 = (bf16[2048,128]{1,0:T(8,128)(2,1)S(1)}, bf16[2048,128]{1,0:T(8,128)(2,1)S(1)}, u32[]{:S(2)}, u32[]{:S(2)}) collective-permute-start(bf16[2048,128]{1,0:T(8,128)(2,1)S(1)} %all_gather.3.far), channel_id=1, source_target_pairs={{0,480},{8,488},{16,496},{24,504},{32,0},{40,8},{48,16},{56,24},{6... | collective-permute-start | bytes 1572872 | tf_op jit(solution)/shard_map/ppermute | solution.py:376
  44.0 16.8 %collective-permute-start.1 = (bf16[2048,128]{1,0:T(8,128)(2,1)S(1)}, bf16[2048,128]{1,0:T(8,128)(2,1)S(1)}, u32[]{:S(2)}, u32[]{:S(2)}) collective-permute-start(bf16[2048,128]{1,0:T(8,128)(2,1)S(1)} %all_gather.3.far), channel_id=1, source_target_pairs={{0,32},{8,40},{16,48},{24,56},{32,64},{40,72},{48,80},{56,88},{64,... | collective-permute-start | bytes 1572872 | tf_op jit(solution)/shard_map/ppermute | solution.py:375
  47.9 26.4 %collective-permute-start.5 = (bf16[2048,128]{1,0:T(8,128)(2,1)S(1)}, bf16[2048,128]{1,0:T(8,128)(2,1)S(1)}, u32[]{:S(2)}, u32[]{:S(2)}) collective-permute-start(bf16[2048,128]{1,0:T(8,128)(2,1)S(1)} %all_gather.3.far), channel_id=1, source_target_pairs={{0,64},{8,456},{16,80},{24,472},{32,96},{40,488},{48,112},{56,504}... | collective-permute-start | bytes 1572872 | tf_op jit(solution)/shard_map/ppermute | solution.py:377
  52.2 1.0 copy-start.1
  53.2 0.9 copy-start.3
  54.1 0.9 copy-start.4
  55.0 5.7 %copy-start.2 = (bf16[2,768,128]{2,1,0:T(8,128)(2,1)S(1)}, bf16[2,768,128]{2,1,0:T(8,128)(2,1)}, u32[]{:S(2)}) copy-start(bf16[2,768,128]{2,1,0:T(8,128)(2,1)} %get-tuple-element.30.q_own) | copy-start | bytes 1179652
  62.5 15.7 %collective-permute-start.4 = (bf16[4096,128]{1,0:T(8,128)(2,1)S(1)}, bf16[4096,128]{1,0:T(8,128)(2,1)S(1)}, u32[]{:S(2)}, u32[]{:S(2)}) collective-permute-start(bf16[4096,128]{1,0:T(8,128)(2,1)S(1)} %get-tuple-element.42), channel_id=1, source_target_pairs={{0,8},{8,0},{16,24},{24,16},{32,40},{40,32},{48,56},{56,48},{64,72... | collective-permute-start | bytes 3145736 | tf_op jit(solution)/shard_map/ppermute | solution.py:397
  74.4 3.8 %collective-permute-start.6 = (bf16[2048,128]{1,0:T(8,128)(2,1)S(1)}, bf16[2048,128]{1,0:T(8,128)(2,1)S(1)}, u32[]{:S(2)}, u32[]{:S(2)}) collective-permute-start(bf16[2048,128]{1,0:T(8,128)(2,1)S(1)} %collective-permute-done.5.refs_0_), channel_id=1, source_target_pairs={{0,8},{8,0},{16,24},{24,16},{32,40},{40,32},{48,56},{56,48},{64,72... | collective-permute-start | bytes 1572872 | tf_op jit(solution)/shard_map/ppermute | solution.py:399
  79.6 10.9 %copy-start = (bf16[384,5120]{1,0:T(8,128)(2,1)S(1)}, bf16[384,5120]{1,0:T(8,128)(2,1)}, u32[]{:S(2)}) copy-start(bf16[384,5120]{1,0:T(8,128)(2,1)} %weight.1) | copy-start | bytes 11796484
  79.6 10.9 %collective-permute-start.7 = (bf16[816,128]{1,0:T(8,128)(2,1)S(1)}, bf16[816,128]{1,0:T(8,128)(2,1)S(1)}, u32[]{:S(2)}, u32[]{:S(2)}) collective-permute-start(bf16[816,128]{1,0:T(8,128)(2,1)S(1)} %shard_map.78), channel_id=1, source_target_pairs={{0,16},{8,24},{16,0},{24,8},{32,48},{40,56},{48,32},{56,40},{64,80... | collective-permute-start | bytes 626696 | tf_op jit(solution)/shard_map/ppermute | solution.py:409

commit v2 on v1

--- a/solution.py
+++ b/solution.py
@@ -55,7 +55,13 @@
     return x * tables[0] + pltpu.roll(x, HEAD_DIM // 2, 1) * tables[1]
 
 
-def prepare_kernel(queries, keys, values, own, succ, inter, kv, q_pair, q_intra):
+def prepare_kernel(queries, keys, values, own, succ, inter, weight, kv, q_pair, q_intra, blocks, sems):
+    width = blocks.shape[2]
+    copies = [
+        pltpu.make_async_copy(weight.at[:, t * width:(t + 1) * width], blocks.at[t], sems.at[t]) for t in range(TP)
+    ]
+    for copy in copies:
+        copy.start()
     own_tables = full_tables(own[...])
     kv[:SPAN, :] = rotated(keys[...].astype(F32), own_tables).astype(BF)
     kv[SPAN:, :] = values[...]
@@ -67,21 +73,28 @@
         q_pair[0, rows, :] = rotated(x, inter_tables).astype(BF)
         q_pair[1, rows, :] = rotated(x, succ_tables).astype(BF)
         q_intra[rows, :] = rotated(x, own_tables).astype(BF)
+    for copy in copies:
+        copy.wait()
 
 
 def prepare(*operands):
     def whole(x):
         return pl.BlockSpec(x.shape, lambda i: (0,) * len(x.shape))
 
-    outs = (shape((2 * SPAN, HEAD_DIM), BF), shape((2, ROWS, HEAD_DIM), BF), shape((ROWS, HEAD_DIM), BF))
+    depth, width = operands[-1].shape[0], operands[-1].shape[1] // TP
+    outs = (
+        shape((2 * SPAN, HEAD_DIM), BF), shape((2, ROWS, HEAD_DIM), BF), shape((ROWS, HEAD_DIM), BF),
+        shape((TP, depth, width), BF),
+    )
     return pl.pallas_call(
         prepare_kernel,
         grid=(1,),
         out_shape=outs,
-        in_specs=[whole(x) for x in operands],
+        in_specs=[whole(x) for x in operands[:-1]] + [pl.BlockSpec(memory_space=pl.ANY)],
         out_specs=tuple(whole(x) for x in outs),
+        scratch_shapes=[pltpu.SemaphoreType.DMA((TP,))],
         compiler_params=pltpu.CompilerParams(vmem_limit_bytes=60 * 1024 * 1024),
-        cost_estimate=pl.CostEstimate(flops=10 ** 6, bytes_accessed=2 ** 20, transcendentals=0),
+        cost_estimate=pl.CostEstimate(flops=10 ** 6, bytes_accessed=2 ** 23, transcendentals=0),
     )(*operands)
 
 
@@ -204,17 +217,25 @@
     absorb_all(targets_of(here), [spans_of(here, 0, False), spans_of(here, 0, True)], lambda i: q_all.at[i], joined, states)
 
 
-def near_kernel(steps, place, q_own, q_peer, before, *refs):
-    bufs, ins, states = refs[:len(steps)], refs[len(steps):len(steps) + 3], refs[len(steps) + 3:len(steps) + 6]
-    done, joined, q_all = refs[len(steps) + 6:]
+def near_kernel(place, q_own, q_peer, before, low, high, *refs):
+    ins, states, (done, joined, q_all) = refs[:3], refs[3:6], refs[6:]
     done[...] = before[...]
     for source, target in zip(ins, states):
         target[...] = source[...]
     q_all[0] = q_own[...]
     q_all[1] = q_peer[...]
-    copy_all(bufs, joined)
+    copy_all([low, high], joined)
     here = place[0]
-    absorb_all(targets_of(here), [spans_of(here, step, False) for step in steps], lambda i: q_all.at[i], joined, states)
+    absorb_all(
+        targets_of(here), [spans_of(here, step, False) for step in STEPS[:2]], lambda i: q_all.at[i], joined, states)
+
+
+def near_peer_kernel(place, q_peer, near, *refs):
+    ins, states = refs[:3], refs[3:6]
+    for source, target in zip(ins, states):
+        target[...] = source[1:2]
+    here = place[0]
+    absorb_all(targets_of(here)[1:], [spans_of(here, STEPS[2], False)], lambda i: q_peer, near, states)
 
 
 def three_terms(x):
@@ -226,16 +247,16 @@
 
 
 def last_segments(place):
-    return [spans_of(place, step, True) for step in STEPS]
+    return [spans_of(place, step, True) for step in STEPS] + [spans_of(place, STEPS[2], False)]
 
 
 def peer_kernel(place, q_peer, two, three, *refs):
     ins, out, state, joined = refs[:3], refs[3], refs[4:7], refs[7]
     for source, target in zip(ins, state):
-        target[0] = source[1]
+        target[...] = source[...]
     copy_all([two, three], joined)
     here = place[0]
-    absorb_all(targets_of(here)[1:], last_segments(here), lambda i: q_peer, joined, state)
+    absorb_all(targets_of(here)[1:], last_segments(here)[:3], lambda i: q_peer, joined, state)
     state = [x.at[0] for x in state]
     lane = lax.broadcasted_iota(jnp.int32, (SPAN, HEAD_DIM), 1)
     for h in range(GROUP):
@@ -252,11 +273,11 @@
         out[ROWS + 16 * h:ROWS + 16 * (h + 1), :] = both.astype(BF)
 
 
-def own_kernel(place, q_own, two, three, *refs):
+def own_kernel(place, q_own, two, three, near, before, *refs):
     ins, outs, joined = refs[:3], refs[3:6], refs[6]
     for source, target in zip(ins, outs):
         target[...] = source[0:1]
-    copy_all([two, three], joined)
+    copy_all([two, three, near], joined)
     here = place[0]
     absorb_all(targets_of(here)[:1], last_segments(here), lambda i: q_own, joined, outs)
 
@@ -279,51 +300,16 @@
         out[:, h * HEAD_DIM:(h + 1) * HEAD_DIM] = value.astype(BF)
 
 
-def project_kernel(top, total, summed, part, weight, out, attended):
-    @pl.when(pl.program_id(0) == 0)
-    def _():
-        merge(top.at[0], total.at[0], summed.at[0], part, attended)
-
-    out[0] = jnp.dot(attended[...], weight[...], preferred_element_type=F32).astype(BF)
-
-
-def project(state, part, weight):
-    depth, width = weight.shape[0], weight.shape[1] // TP
-    whole = pl.BlockSpec((1, ROWS, HEAD_DIM), lambda t: (0, 0, 0))
-    return pl.pallas_call(
-        project_kernel,
-        grid=(TP,),
-        out_shape=shape((TP, SPAN, width), BF),
-        in_specs=[whole] * 3 + [
-            pl.BlockSpec((PART_ROWS, HEAD_DIM), lambda t: (0, 0)), pl.BlockSpec((depth, width), lambda t: (0, t))
-        ],
-        out_specs=pl.BlockSpec((1, SPAN, width), lambda t: (t, 0, 0)),
-        scratch_shapes=[pltpu.VMEM((SPAN, depth), BF)],
-        compiler_params=pltpu.CompilerParams(vmem_limit_bytes=16 * 1024 * 1024),
-        cost_estimate=pl.CostEstimate(
-            flops=2 * SPAN * depth * TP * width, bytes_accessed=2 * TP * width * (depth + SPAN), transcendentals=0),
-    )(*state, part, weight)
-
-
-def sum_kernel(parts, out):
-    total = parts[0].astype(F32)
-    for t in range(1, TP):
-        total = total + parts[t].astype(F32)
+def merge_kernel(top, total, summed, part, out, attended):
+    merge(top.at[0], total.at[0], summed.at[0], part, attended)
+    for t in range(TP):
+        out[t] = attended[...]
+
+
+def project_kernel(attended, weight, out):
+    rows = jnp.concatenate([attended[t] for t in range(TP)], axis=1)
+    total = jnp.dot(rows, weight[...].reshape(rows.shape[1], out.shape[1]), preferred_element_type=F32)
     out[...] = total.astype(BF)
-
-
-def sum_parts(parts):
-    _, rows, width = parts.shape
-    block = rows // 4
-    return pl.pallas_call(
-        sum_kernel,
-        grid=(4,),
-        out_shape=shape((rows, width), BF),
-        in_specs=[pl.BlockSpec((TP, block, width), lambda t: (0, t, 0))],
-        out_specs=pl.BlockSpec((block, width), lambda t: (t, 0)),
-        compiler_params=pltpu.CompilerParams(vmem_limit_bytes=12 * 1024 * 1024),
-        cost_estimate=pl.CostEstimate(flops=TP * rows * width, bytes_accessed=2 * TP * rows * width, transcendentals=0),
-    )(parts)
 
 
 def call(kernel, outs, operands, flops, scratch=(), smem_first=True):
@@ -367,16 +353,18 @@
     own_table, succ_table, inter_table = (jnp.asarray(t) for t in rope_tables())
     place = lax.axis_index("ctx").astype(jnp.int32).reshape(1)
 
-    kv, q_own, q_intra = prepare(queries, keys, values, own_table, succ_table, inter_table)
+    kv, q_own, q_intra, blocks = prepare(queries, keys, values, own_table, succ_table, inter_table, out_weight)
     q_peer = lax.ppermute(q_own, "ctx", SWAP_HI)
     far = lax.all_gather(kv, "ctx", axis=0, tiled=True, axis_index_groups=FAR_GROUPS)
-    far, q_peer = lax.optimization_barrier((far, q_peer))
+    far, q_peer, blocks = lax.optimization_barrier((far, q_peer, blocks))
+    weight = lax.all_to_all(blocks, "tp", 0, 0)
     near = [
         lax.ppermute(far, "ctx", z_route(1, 1)),
         lax.ppermute(far, "ctx", z_route(-1, -1)),
         lax.ppermute(far, "ctx", z_route(2, -2)),
     ]
     far_other = lax.ppermute(far, "ctx", SWAP_CORE)
+    far_other, *near[:2] = lax.optimization_barrier((far_other, *near[:2]))
 
     state_shapes = [shape((1, ROWS, HEAD_DIM), F32)] * 3
     both_shapes = [shape((2, ROWS, HEAD_DIM), F32)] * 3
@@ -389,27 +377,34 @@
         first_kernel, both_shapes + [token], [place, q_own, q_peer, q_intra, kv, far, far_other], 17 * tile,
         scratch=[q_scratch, pltpu.VMEM((2 * size, HEAD_DIM), BF)],
     )
-    *near[:2], done = lax.optimization_barrier((*near[:2], done))
     *state, done, joined = call(
-        functools.partial(near_kernel, STEPS[:2]), both_shapes + [token, shape((2 * size, HEAD_DIM), BF)],
+        near_kernel, both_shapes + [token, shape((2 * size, HEAD_DIM), BF)],
         [place, q_own, q_peer, done] + near[:2] + state, 16 * tile, scratch=[q_scratch],
     )
     two = lax.ppermute(joined, "ctx", SWAP_CORE)
-    near[2], done = lax.optimization_barrier((near[2], done))
-    three = lax.ppermute(near[2], "ctx", SWAP_CORE)
-    *state, _, _ = call(
-        functools.partial(near_kernel, STEPS[2:]), both_shapes + [token, shape((size, HEAD_DIM), BF)],
-        [place, q_own, q_peer, done] + near[2:] + state, 8 * tile, scratch=[q_scratch],
-    )
-    last_scratch = pltpu.VMEM((3 * size, HEAD_DIM), BF)
+    third, done = lax.optimization_barrier((near[2], done))
+    three = lax.ppermute(third, "ctx", SWAP_CORE)
+    peers = call(near_peer_kernel, state_shapes, [place, q_peer, third] + state, 4 * tile)
     (part,) = call(
-        peer_kernel, [shape((PART_ROWS, HEAD_DIM), BF)], [place, q_peer, two, three] + state, 12 * tile,
-        scratch=[pltpu.VMEM((1, ROWS, HEAD_DIM), F32)] * 3 + [last_scratch],
+        peer_kernel, [shape((PART_ROWS, HEAD_DIM), BF)], [place, q_peer, two, three] + list(peers), 12 * tile,
+        scratch=[pltpu.VMEM((1, ROWS, HEAD_DIM), F32)] * 3 + [pltpu.VMEM((3 * size, HEAD_DIM), BF)],
     )
     part_here = lax.ppermute(part, "ctx", SWAP_HI)
-    own = call(own_kernel, state_shapes, [place, q_own, two, three] + state, 12 * tile, scratch=[last_scratch])
-    partial = project(own, part_here, out_weight)
-    return sum_parts(lax.all_to_all(partial, "tp", 0, 0))
+    own = call(
+        own_kernel, state_shapes, [place, q_own, two, three, third, done] + state, 16 * tile,
+        scratch=[pltpu.VMEM((4 * size, HEAD_DIM), BF)],
+    )
+    (attended,) = call(
+        merge_kernel, [shape((TP, SPAN, GROUP * HEAD_DIM), BF)], list(own) + [part_here], 10 ** 6, smem_first=False,
+        scratch=[pltpu.VMEM((SPAN, GROUP * HEAD_DIM), BF)],
+    )
+    attended, weight = lax.optimization_barrier((attended, weight))
+    attended = lax.all_to_all(attended, "tp", 0, 0)
+    depth, width = weight.shape[1:]
+    (out,) = call(
+        project_kernel, [shape((SPAN, width), BF)], [attended, weight], 2 * SPAN * depth * TP * width, smem_first=False
+    )
+    return out
 
 
 def solution(mesh):

time: 133 us -> 128 us (0.962)
  the two profiles are of different devices: /device:TPU:32 before, /device:TPU:256 now
where the time goes in v2:
time: 128 us; the launch traced here: 127 us
  blocking collectives  52.4 us (41%)
  Pallas kernels  32.9 us (26%)
  starting transfers between devices  32.2 us (25%)
  waiting for transfers between devices  9.45 us (7%)
    all_to_all x1, blocking collectives, local(): attended = lax.all_to_all(attended, 'tp', 0, 0)  28.3 us
    pallas_call x7, Pallas kernels, call(): pl.pallas_call(kernel, out_shape=tuple(outs), in_specs=specs, out_specs=t...  27.5 us
    all_gather x1, blocking collectives, local(): lax.all_gather(kv, 'ctx', axis=0, tiled=True, axis_index_groups=FAR_GROUPS)  24.1 us
    ppermute x1, waiting for transfers between devices, local(): lax.ppermute(far, 'ctx', z_route(1, 1))  7.05 us
    ppermute x1, starting transfers between devices, local(): part_here = lax.ppermute(part, 'ctx', SWAP_HI)  5.68 us
    pallas_call x1, Pallas kernels, prepare(): pl.pallas_call(prepare_kernel, grid=(1,), out_shape=outs, in_specs=[whole...  5.38 us
    ppermute x1, starting transfers between devices, local(): q_peer = lax.ppermute(q_own, 'ctx', SWAP_HI)  4.93 us
    ppermute x1, starting transfers between devices, local(): lax.ppermute(far, 'ctx', z_route(-1, -1))  4.74 us
  transfers between devices with their start and end apart: 9, of which 4 were waited for; matrix products, arithmetic and copies ran while one was open for 0% of the time, Pallas kernels for 18%

profile of v2, /device:TPU:256, one launch (start us, length us, event | category | flops | bytes accessed | tf_op | source)
XLA Modules:
  0.0 127.1 jit_solution(15954663286363946218)
XLA Ops:
  0.0 5.4 %shard_map.73 = (bf16[512,128]{1,0:T(8,128)(2,1)}, bf16[2,768,128]{2,1,0:T(8,128)(2,1)}, bf16[768,128]{1,0:T(8,128)(2,1)}, bf16[8,384,640]{2,1,0:T(8,128)(2,1)}) custom-call(bf16[256,384]{1,0:T(8,128)(2,1)} %queries.1, bf16[256,128]{1,0:T(8,128)(2,1)} %keys.1, bf16[256,128]{1,0:T(8,128)(2,1)} %values.1, f32[256,128]{1,0:T(8,128)} %constant.12.clone.own, ...), custom_call_target="tpu_custom_call" | custom-call | flops 1000000 | bytes 8388608 | tf_op jit(solution)/shard_map/pallas_call | solution.py:89
  5.4 4.9 %collective-permute-start = (bf16[2,768,128]{2,1,0:T(8,128)(2,1)}, bf16[2,768,128]{2,1,0:T(8,128)(2,1)S(1)}, u32[]{:S(2)}, u32[]{:S(2)}) collective-permute-start(bf16[2,768,128]{2,1,0:T(8,128)(2,1)} %get-tuple-element.34.q_own), channel_id=1, source_target_pairs={{0,16},{8,24},{16,0},{24,8},{32,48},{40,56},{48,32},{56,40},{64,80... | collective-permute-start | bytes 1179656 | tf_op jit(solution)/shard_map/ppermute | solution.py:357
  10.3 24.1 %all_gather.3.far = bf16[2048,128]{1,0:T(8,128)(2,1)S(1)} all-gather(bf16[512,128]{1,0:T(8,128)(2,1)} %get-tuple-element.35.kv), channel_id=1, replica_groups={{0,128,256,384},{392,264,136,8},{16,144,272,400},{408,280,152,24},{32,1..., dimensions={0}, use_global_device_ids=true | all-gather | bytes 655360 | tf_op jit(solution)/shard_map/all_gather | solution.py:358
  34.4 0.0 copy-start.2
  34.4 4.7 %all-to-all-start = ((bf16[8,384,640]{2,1,0:T(8,128)(2,1)}), bf16[8,384,640]{2,1,0:T(8,128)(2,1)}, u32[]{:S(2)}, u32[]{:S(2)}) async-start(bf16[8,384,640]{2,1,0:T(8,128)(2,1)} %get-tuple-element.60), calls=%async_computation | async-start | bytes 7864320 | tf_op jit(solution)/shard_map/all_to_all | solution.py:360
  39.1 4.7 %collective-permute-start.3 = (bf16[2048,128]{1,0:T(8,128)(2,1)S(1)}, bf16[2048,128]{1,0:T(8,128)(2,1)S(1)}, u32[]{:S(2)}, u32[]{:S(2)}) collective-permute-start(bf16[2048,128]{1,0:T(8,128)(2,1)S(1)} %all_gather.3.far), channel_id=1, source_target_pairs={{0,480},{8,488},{16,496},{24,504},{32,0},{40,8},{48,16},{56,24},{6... | collective-permute-start | bytes 1572872 | tf_op jit(solution)/shard_map/ppermute | solution.py:363
  43.9 1.9 %collective-permute-start.2 = (bf16[2048,128]{1,0:T(8,128)(2,1)S(1)}, bf16[2048,128]{1,0:T(8,128)(2,1)S(1)}, u32[]{:S(2)}, u32[]{:S(2)}) collective-permute-start(bf16[2048,128]{1,0:T(8,128)(2,1)S(1)} %all_gather.3.far), channel_id=1, source_target_pairs={{0,32},{8,40},{16,48},{24,56},{32,64},{40,72},{48,80},{56,88},{64,... | collective-permute-start | bytes 1572872 | tf_op jit(solution)/shard_map/ppermute | solution.py:362
  45.8 1.9 %collective-permute-start.1 = (bf16[2048,128]{1,0:T(8,128)(2,1)S(1)}, bf16[2048,128]{1,0:T(8,128)(2,1)S(1)}, u32[]{:S(2)}, u32[]{:S(2)}) collective-permute-start(bf16[2048,128]{1,0:T(8,128)(2,1)S(1)} %all_gather.3.far), channel_id=1, source_target_pairs={{0,8},{8,0},{16,24},{24,16},{32,40},{40,32},{48,56},{56,48},{64,72... | collective-permute-start | bytes 1572872 | tf_op jit(solution)/shard_map/ppermute | solution.py:366
  47.7 4.0 %collective-permute-start.5 = (bf16[2048,128]{1,0:T(8,128)(2,1)S(1)}, bf16[2048,128]{1,0:T(8,128)(2,1)S(1)}, u32[]{:S(2)}, u32[]{:S(2)}) collective-permute-start(bf16[2048,128]{1,0:T(8,128)(2,1)S(1)} %all_gather.3.far), channel_id=1, source_target_pairs={{0,64},{8,456},{16,80},{24,472},{32,96},{40,488},{48,112},{56,504}... | collective-permute-start | bytes 1572872 | tf_op jit(solution)/shard_map/ppermute | solution.py:364
  51.7 1.8 %collective-permute-done.3.high = bf16[2048,128]{1,0:T(8,128)(2,1)S(1)} collective-permute-done((bf16[2048,128]{1,0:T(8,128)(2,1)S(1)}, bf16[2048,128]{1,0:T(8,128)(2,1)S(1)}, u32[]{:S(2)}, u32[]{:S(2)}) %collective-permute-start.3) | collective-permute-done | bytes 524320 | tf_op jit(solution)/shard_map/ppermute | solution.py:363
  53.5 7.0 %collective-permute-done.2.low = bf16[2048,128]{1,0:T(8,128)(2,1)S(1)} collective-permute-done((bf16[2048,128]{1,0:T(8,128)(2,1)S(1)}, bf16[2048,128]{1,0:T(8,128)(2,1)S(1)}, u32[]{:S(2)}, u32[]{:S(2)}) %collective-permute-start.2) | collective-permute-done | bytes 524320 | tf_op jit(solution)/shard_map/ppermute | solution.py:362
  60.6 6.3 %shard_map.74 = (f32[2,768,128]{2,1,0:T(8,128)S(1)}, f32[2,768,128]{2,1,0:T(8,128)S(1)}, f32[2,768,128]{2,1,0:T(8,128)S(1)}, f32[8,128]{1,0:T(8,128)S(1)}) custom-call(s32[1]{0:T(128)} %bitcast.place, bf16[2,768,128]{2,1,0:T(8,128)(2,1)S(1)} %copy-done.1, bf16[2,768,128]{2,1,0:T(8,128)(2,1)S(1)} %collective-permute-done.q_peer, ...), custom_call_target="tpu_custom_call" | custom-call | flops 1711276032 | bytes 4526084 | tf_op jit(solution)/shard_map/pallas_call | solution.py:320
  66.9 5.2 %shard_map.75 = (f32[2,768,128]{2,1,0:T(8,128)S(1)}, f32[2,768,128]{2,1,0:T(8,128)S(1)}, f32[2,768,128]{2,1,0:T(8,128)S(1)}, f32[8,128]{1,0:T(8,128)S(1)}, bf16[4096,128]{1,0:T(8,128)(2,1)S(1)}) custom-call(s32[1]{0:T(128)} %bitcast.place, bf16[2,768,128]{2,1,0:T(8,128)(2,1)S(1)} %copy-done.1, bf16[2,768,128]{2,1,0:T(8,128)(2,1)S(1)} %collective-permute-done.q_peer, ...), custom_call_target="tpu_custom_call" | custom-call | flops 1610612736 | bytes 7610372 | tf_op jit(solution)/shard_map/pallas_call | solution.py:320
  72.1 1.9 %collective-permute-start.4 = (bf16[4096,128]{1,0:T(8,128)(2,1)S(1)}, bf16[4096,128]{1,0:T(8,128)(2,1)S(1)}, u32[]{:S(2)}, u32[]{:S(2)}) collective-permute-start(bf16[4096,128]{1,0:T(8,128)(2,1)S(1)} %get-tuple-element.47), channel_id=1, source_target_pairs={{0,8},{8,0},{16,24},{24,16},{32,40},{40,32},{48,56},{56,48},{64,72... | collective-permute-start | bytes 3145736 | tf_op jit(solution)/shard_map/ppermute | solution.py:384
  74.0 2.4 %collective-permute-start.6 = (bf16[2048,128]{1,0:T(8,128)(2,1)S(1)}, bf16[2048,128]{1,0:T(8,128)(2,1)S(1)}, u32[]{:S(2)}, u32[]{:S(2)}) collective-permute-start(bf16[2048,128]{1,0:T(8,128)(2,1)S(1)} %collective-permute-done.5.near), channel_id=1, source_target_pairs={{0,8},{8,0},{16,24},{24,16},{32,40},{40,32},{48,56},{56,48},{64,72... | collective-permute-start | bytes 1572872 | tf_op jit(solution)/shard_map/ppermute | solution.py:386
  76.4 1.4 %shard_map.77 = (f32[1,768,128]{2,1,0:T(8,128)S(1)}, f32[1,768,128]{2,1,0:T(8,128)S(1)}, f32[1,768,128]{2,1,0:T(8,128)S(1)}) custom-call(s32[1]{0:T(128)} %bitcast.place, bf16[2,768,128]{2,1,0:T(8,128)(2,1)S(1)} %collective-permute-done.q_peer, bf16[2048,128]{1,0:T(8,128)(2,1)S(1)} %collective-permute-done.5.near, ...), custom_call_target="tpu_custom_call" | custom-call | flops 402653184 | bytes 4456452 | tf_op jit(solution)/shard_map/pallas_call | solution.py:320
  77.9 0.1 collective-permute-done.6.three
  78.0 4.2 %shard_map.78 = bf16[816,128]{1,0:T(8,128)(2,1)S(1)} custom-call(s32[1]{0:T(128)} %bitcast.place, bf16[2,768,128]{2,1,0:T(8,128)(2,1)S(1)} %collective-permute-done.q_peer, bf16[4096,128]{1,0:T(8,128)(2,1)S(1)} %collective-permute-done.4.two, bf16[2048,128]{1,0:T(8,128)(2,1)S(1)} %collective-permute-done.6.three, ...), custom_call_target="tpu_custom_call" | custom-call | flops 1207959552 | bytes 3354628 | tf_op jit(solution)/shard_map/pallas_call | solution.py:320
  82.2 5.7 %collective-permute-start.7 = (bf16[816,128]{1,0:T(8,128)(2,1)S(1)}, bf16[816,128]{1,0:T(8,128)(2,1)S(1)}, u32[]{:S(2)}, u32[]{:S(2)}) collective-permute-start(bf16[816,128]{1,0:T(8,128)(2,1)S(1)} %shard_map.78), channel_id=1, source_target_pairs={{0,16},{8,24},{16,0},{24,8},{32,48},{40,56},{48,32},{56,40},{64,80... | collective-permute-start | bytes 626696 | tf_op jit(solution)/shard_map/ppermute | solution.py:392
  87.9 5.1 %shard_map.76 = (f32[1,768,128]{2,1,0:T(8,128)S(1)}, f32[1,768,128]{2,1,0:T(8,128)S(1)}, f32[1,768,128]{2,1,0:T(8,128)S(1)}) custom-call(s32[1]{0:T(128)} %bitcast.place, bf16[2,768,128]{2,1,0:T(8,128)(2,1)S(1)} %copy-done.1, bf16[4096,128]{1,0:T(8,128)(2,1)S(1)} %collective-permute-done.4.two, bf16[2048,128]{1,0:T(8,128)(2,1)S(1)} %collective-permute-done.6.three, ...), custom_call_target="tpu_custom_call" | custom-call | flops 1610612736 | bytes 6033412 | tf_op jit(solution)/shard_map/pallas_call | solution.py:320
  93.0 0.5 collective-permute-done.7.part
  93.5 1.0 shard_map.79
  94.5 28.3 %all_to_all.10.attended = bf16[8,256,384]{2,1,0:T(8,128)(2,1)S(1)} all-to-all(bf16[8,256,384]{2,1,0:T(8,128)(2,1)S(1)} %shard_map.79), channel_id=1, replica_groups=mesh['ctx'=64,'tp'=8] {'tp'}, dimensions={0} | all-to-all | bytes 3145728 | tf_op jit(solution)/shard_map/all_to_all | solution.py:402
  122.8 4.2 %shard_map.80 = bf16[256,640]{1,0:T(8,128)(2,1)} custom-call(bf16[8,256,384]{2,1,0:T(8,128)(2,1)S(1)} %all_to_all.10.attended, bf16[8,384,640]{2,1,0:T(8,128)(2,1)} %all-to-all-done.weight), custom_call_target="tpu_custom_call" | custom-call | flops 1006632960 | bytes 5832704 | tf_op jit(solution)/shard_map/pallas_call | solution.py:320
  (10 shorter events, 0.0 us)
Async XLA Ops:
  5.4 29.0 %collective-permute-start = (bf16[2,768,128]{2,1,0:T(8,128)(2,1)}, bf16[2,768,128]{2,1,0:T(8,128)(2,1)S(1)}, u32[]{:S(2)}, u32[]{:S(2)}) collective-permute-start(bf16[2,768,128]{2,1,0:T(8,128)(2,1)} %get-tuple-element.34.q_own), channel_id=1, source_target_pairs={{0,16},{8,24},{16,0},{24,8},{32,48},{40,56},{48,32},{56,40},{64,80... | collective-permute-start | bytes 1179656 | tf_op jit(solution)/shard_map/ppermute | solution.py:357
  34.4 26.2 %copy-start = (bf16[512,128]{1,0:T(8,128)(2,1)S(1)}, bf16[512,128]{1,0:T(8,128)(2,1)}, u32[]{:S(2)}) copy-start(bf16[512,128]{1,0:T(8,128)(2,1)} %get-tuple-element.35.kv) | copy-start | bytes 393220
  34.4 26.2 %copy-start.1 = (bf16[2,768,128]{2,1,0:T(8,128)(2,1)S(1)}, bf16[2,768,128]{2,1,0:T(8,128)(2,1)}, u32[]{:S(2)}) copy-start(bf16[2,768,128]{2,1,0:T(8,128)(2,1)} %get-tuple-element.34.q_own) | copy-start | bytes 1179652
  34.4 26.2 %copy-start.2 = (bf16[768,128]{1,0:T(8,128)(2,1)S(1)}, bf16[768,128]{1,0:T(8,128)(2,1)}, u32[]{:S(2)}) copy-start(bf16[768,128]{1,0:T(8,128)(2,1)} %get-tuple-element.38.q_intra) | copy-start | bytes 589828
  34.4 60.1 %all-to-all-start = ((bf16[8,384,640]{2,1,0:T(8,128)(2,1)}), bf16[8,384,640]{2,1,0:T(8,128)(2,1)}, u32[]{:S(2)}, u32[]{:S(2)}) async-start(bf16[8,384,640]{2,1,0:T(8,128)(2,1)} %get-tuple-element.60), calls=%async_computation | async-start | bytes 7864320 | tf_op jit(solution)/shard_map/all_to_all | solution.py:360
  39.1 14.4 %collective-permute-start.3 = (bf16[2048,128]{1,0:T(8,128)(2,1)S(1)}, bf16[2048,128]{1,0:T(8,128)(2,1)S(1)}, u32[]{:S(2)}, u32[]{:S(2)}) collective-permute-start(bf16[2048,128]{1,0:T(8,128)(2,1)S(1)} %all_gather.3.far), channel_id=1, source_target_pairs={{0,480},{8,488},{16,496},{24,504},{32,0},{40,8},{48,16},{56,24},{6... | collective-permute-start | bytes 1572872 | tf_op jit(solution)/shard_map/ppermute | solution.py:363
  43.9 16.7 %collective-permute-start.2 = (bf16[2048,128]{1,0:T(8,128)(2,1)S(1)}, bf16[2048,128]{1,0:T(8,128)(2,1)S(1)}, u32[]{:S(2)}, u32[]{:S(2)}) collective-permute-start(bf16[2048,128]{1,0:T(8,128)(2,1)S(1)} %all_gather.3.far), channel_id=1, source_target_pairs={{0,32},{8,40},{16,48},{24,56},{32,64},{40,72},{48,80},{56,88},{64,... | collective-permute-start | bytes 1572872 | tf_op jit(solution)/shard_map/ppermute | solution.py:362
  45.8 14.8 %collective-permute-start.1 = (bf16[2048,128]{1,0:T(8,128)(2,1)S(1)}, bf16[2048,128]{1,0:T(8,128)(2,1)S(1)}, u32[]{:S(2)}, u32[]{:S(2)}) collective-permute-start(bf16[2048,128]{1,0:T(8,128)(2,1)S(1)} %all_gather.3.far), channel_id=1, source_target_pairs={{0,8},{8,0},{16,24},{24,16},{32,40},{40,32},{48,56},{56,48},{64,72... | collective-permute-start | bytes 1572872 | tf_op jit(solution)/shard_map/ppermute | solution.py:366
  47.7 26.3 %collective-permute-start.5 = (bf16[2048,128]{1,0:T(8,128)(2,1)S(1)}, bf16[2048,128]{1,0:T(8,128)(2,1)S(1)}, u32[]{:S(2)}, u32[]{:S(2)}) collective-permute-start(bf16[2048,128]{1,0:T(8,128)(2,1)S(1)} %all_gather.3.far), channel_id=1, source_target_pairs={{0,64},{8,456},{16,80},{24,472},{32,96},{40,488},{48,112},{56,504}... | collective-permute-start | bytes 1572872 | tf_op jit(solution)/shard_map/ppermute | solution.py:364
  72.1 5.9 %collective-permute-start.4 = (bf16[4096,128]{1,0:T(8,128)(2,1)S(1)}, bf16[4096,128]{1,0:T(8,128)(2,1)S(1)}, u32[]{:S(2)}, u32[]{:S(2)}) collective-permute-start(bf16[4096,128]{1,0:T(8,128)(2,1)S(1)} %get-tuple-element.47), channel_id=1, source_target_pairs={{0,8},{8,0},{16,24},{24,16},{32,40},{40,32},{48,56},{56,48},{64,72... | collective-permute-start | bytes 3145736 | tf_op jit(solution)/shard_map/ppermute | solution.py:384
  74.0 3.9 %collective-permute-start.6 = (bf16[2048,128]{1,0:T(8,128)(2,1)S(1)}, bf16[2048,128]{1,0:T(8,128)(2,1)S(1)}, u32[]{:S(2)}, u32[]{:S(2)}) collective-permute-start(bf16[2048,128]{1,0:T(8,128)(2,1)S(1)} %collective-permute-done.5.near), channel_id=1, source_target_pairs={{0,8},{8,0},{16,24},{24,16},{32,40},{40,32},{48,56},{56,48},{64,72... | collective-permute-start | bytes 1572872 | tf_op jit(solution)/shard_map/ppermute | solution.py:386
  82.2 11.3 %collective-permute-start.7 = (bf16[816,128]{1,0:T(8,128)(2,1)S(1)}, bf16[816,128]{1,0:T(8,128)(2,1)S(1)}, u32[]{:S(2)}, u32[]{:S(2)}) collective-permute-start(bf16[816,128]{1,0:T(8,128)(2,1)S(1)} %shard_map.78), channel_id=1, source_target_pairs={{0,16},{8,24},{16,0},{24,8},{32,48},{40,56},{48,32},{56,40},{64,80... | collective-permute-start | bytes 626696 | tf_op jit(solution)/shard_map/ppermute | solution.py:392

commit v3 on v2

--- a/solution.py
+++ b/solution.py
@@ -201,7 +201,7 @@
         at += source.shape[0]
 
 
-def first_kernel(place, q_own, q_peer, q_intra, kv, far, far_other, top, total, summed, done, q_all, joined):
+def first_kernel(place, q_own, q_peer, q_intra, kv, far, top, total, summed, done, q_all):
     done[...] = jnp.zeros(done.shape, F32)
     states = (top, total, summed)
     top[...] = jnp.full(top.shape, FLOOR, F32)
@@ -209,25 +209,25 @@
     summed[...] = jnp.zeros(summed.shape, F32)
     q_all[0] = q_own[...]
     q_all[1] = q_peer[...]
-    copy_all([far, far_other], joined)
     row = lax.broadcasted_iota(jnp.int32, (ROWS, SPAN), 0) % SPAN
     column = lax.broadcasted_iota(jnp.int32, (ROWS, SPAN), 1)
     absorb([x.at[0] for x in states], q_intra, kv[:SPAN, :], kv[SPAN:, :], mask=row >= column)
     here = place[0]
-    absorb_all(targets_of(here), [spans_of(here, 0, False), spans_of(here, 0, True)], lambda i: q_all.at[i], joined, states)
-
-
-def near_kernel(place, q_own, q_peer, before, low, high, *refs):
-    ins, states, (done, joined, q_all) = refs[:3], refs[3:6], refs[6:]
+    absorb_all(targets_of(here), [spans_of(here, 0, False)], lambda i: q_all.at[i], far, states)
+
+
+def near_kernel(place, q_own, q_peer, before, low, high, far_other, *refs):
+    ins, states, (done, joined, q_all, buffers) = refs[:3], refs[3:6], refs[6:]
     done[...] = before[...]
     for source, target in zip(ins, states):
         target[...] = source[...]
     q_all[0] = q_own[...]
     q_all[1] = q_peer[...]
     copy_all([low, high], joined)
+    copy_all([low, high, far_other], buffers)
     here = place[0]
-    absorb_all(
-        targets_of(here), [spans_of(here, step, False) for step in STEPS[:2]], lambda i: q_all.at[i], joined, states)
+    segments = [spans_of(here, step, False) for step in STEPS[:2]] + [spans_of(here, 0, True)]
+    absorb_all(targets_of(here), segments, lambda i: q_all.at[i], buffers, states)
 
 
 def near_peer_kernel(place, q_peer, near, *refs):
@@ -364,7 +364,8 @@
         lax.ppermute(far, "ctx", z_route(2, -2)),
     ]
     far_other = lax.ppermute(far, "ctx", SWAP_CORE)
-    far_other, *near[:2] = lax.optimization_barrier((far_other, *near[:2]))
+
+    kv, *near[:2] = lax.optimization_barrier((kv, *near[:2]))
 
     state_shapes = [shape((1, ROWS, HEAD_DIM), F32)] * 3
     both_shapes = [shape((2, ROWS, HEAD_DIM), F32)] * 3
@@ -374,12 +375,12 @@
     q_scratch = pltpu.VMEM((2, 2, ROWS, HEAD_DIM), BF)
 
     *state, done = call(
-        first_kernel, both_shapes + [token], [place, q_own, q_peer, q_intra, kv, far, far_other], 17 * tile,
-        scratch=[q_scratch, pltpu.VMEM((2 * size, HEAD_DIM), BF)],
-    )
+        first_kernel, both_shapes + [token], [place, q_own, q_peer, q_intra, kv, far], 9 * tile, scratch=[q_scratch])
+    far_other, done = lax.optimization_barrier((far_other, done))
     *state, done, joined = call(
         near_kernel, both_shapes + [token, shape((2 * size, HEAD_DIM), BF)],
-        [place, q_own, q_peer, done] + near[:2] + state, 16 * tile, scratch=[q_scratch],
+        [place, q_own, q_peer, done] + near[:2] + [far_other] + state, 24 * tile,
+        scratch=[q_scratch, pltpu.VMEM((3 * size, HEAD_DIM), BF)],
     )
     two = lax.ppermute(joined, "ctx", SWAP_CORE)
     third, done = lax.optimization_barrier((near[2], done))

time: 128 us -> 127 us (level)
  no operation moved by 1% of the time
where the time goes in v3:
time: 127 us
  blocking collectives  52.4 us (41%)
  Pallas kernels  32.7 us (26%)
  starting transfers between devices  32.2 us (25%)
  waiting for transfers between devices  9.43 us (7%)
    all_to_all x1, blocking collectives, local(): attended = lax.all_to_all(attended, 'tp', 0, 0)  28.3 us
    pallas_call x7, Pallas kernels, call(): pl.pallas_call(kernel, out_shape=tuple(outs), in_specs=specs, out_specs=t...  27.4 us
    all_gather x1, blocking collectives, local(): lax.all_gather(kv, 'ctx', axis=0, tiled=True, axis_index_groups=FAR_GROUPS)  24.1 us
    ppermute x1, waiting for transfers between devices, local(): lax.ppermute(far, 'ctx', z_route(1, 1))  7.05 us
    ppermute x1, starting transfers between devices, local(): part_here = lax.ppermute(part, 'ctx', SWAP_HI)  5.7 us
    pallas_call x1, Pallas kernels, prepare(): pl.pallas_call(prepare_kernel, grid=(1,), out_shape=outs, in_specs=[whole...  5.38 us
    ppermute x1, starting transfers between devices, local(): q_peer = lax.ppermute(q_own, 'ctx', SWAP_HI)  4.93 us
    ppermute x1, starting transfers between devices, local(): lax.ppermute(far, 'ctx', z_route(-1, -1))  4.74 us
  transfers between devices with their start and end apart: 9, of which 4 were waited for; matrix products, arithmetic and copies ran while one was open for 0% of the time, Pallas kernels for 18%

profile of v3, /device:TPU:256, one launch (start us, length us, event | category | flops | bytes accessed | tf_op | source)
XLA Modules:
  0.0 126.9 jit_solution(8554579526603647343)
XLA Ops:
  0.0 5.4 %shard_map.73 = (bf16[512,128]{1,0:T(8,128)(2,1)}, bf16[2,768,128]{2,1,0:T(8,128)(2,1)}, bf16[768,128]{1,0:T(8,128)(2,1)}, bf16[8,384,640]{2,1,0:T(8,128)(2,1)}) custom-call(bf16[256,384]{1,0:T(8,128)(2,1)} %queries.1, bf16[256,128]{1,0:T(8,128)(2,1)} %keys.1, bf16[256,128]{1,0:T(8,128)(2,1)} %values.1, f32[256,128]{1,0:T(8,128)} %constant.12.clone.own, ...), custom_call_target="tpu_custom_call" | custom-call | flops 1000000 | bytes 8388608 | tf_op jit(solution)/shard_map/pallas_call | solution.py:89
  5.4 4.9 %collective-permute-start = (bf16[2,768,128]{2,1,0:T(8,128)(2,1)}, bf16[2,768,128]{2,1,0:T(8,128)(2,1)S(1)}, u32[]{:S(2)}, u32[]{:S(2)}) collective-permute-start(bf16[2,768,128]{2,1,0:T(8,128)(2,1)} %get-tuple-element.36.q_own), channel_id=1, source_target_pairs={{0,16},{8,24},{16,0},{24,8},{32,48},{40,56},{48,32},{56,40},{64,80... | collective-permute-start | bytes 1179656 | tf_op jit(solution)/shard_map/ppermute | solution.py:357
  10.3 24.1 %all_gather.3.far = bf16[2048,128]{1,0:T(8,128)(2,1)S(1)} all-gather(bf16[512,128]{1,0:T(8,128)(2,1)} %get-tuple-element.42.kv), channel_id=1, replica_groups={{0,128,256,384},{392,264,136,8},{16,144,272,400},{408,280,152,24},{32,1..., dimensions={0}, use_global_device_ids=true | all-gather | bytes 655360 | tf_op jit(solution)/shard_map/all_gather | solution.py:358
  34.4 0.0 copy-start.2
  34.4 4.7 %all-to-all-start = ((bf16[8,384,640]{2,1,0:T(8,128)(2,1)}), bf16[8,384,640]{2,1,0:T(8,128)(2,1)}, u32[]{:S(2)}, u32[]{:S(2)}) async-start(bf16[8,384,640]{2,1,0:T(8,128)(2,1)} %get-tuple-element.64), calls=%async_computation | async-start | bytes 7864320 | tf_op jit(solution)/shard_map/all_to_all | solution.py:360
  39.1 4.7 %collective-permute-start.3 = (bf16[2048,128]{1,0:T(8,128)(2,1)S(1)}, bf16[2048,128]{1,0:T(8,128)(2,1)S(1)}, u32[]{:S(2)}, u32[]{:S(2)}) collective-permute-start(bf16[2048,128]{1,0:T(8,128)(2,1)S(1)} %all_gather.3.far), channel_id=1, source_target_pairs={{0,480},{8,488},{16,496},{24,504},{32,0},{40,8},{48,16},{56,24},{6... | collective-permute-start | bytes 1572872 | tf_op jit(solution)/shard_map/ppermute | solution.py:363
  43.9 1.9 %collective-permute-start.2 = (bf16[2048,128]{1,0:T(8,128)(2,1)S(1)}, bf16[2048,128]{1,0:T(8,128)(2,1)S(1)}, u32[]{:S(2)}, u32[]{:S(2)}) collective-permute-start(bf16[2048,128]{1,0:T(8,128)(2,1)S(1)} %all_gather.3.far), channel_id=1, source_target_pairs={{0,32},{8,40},{16,48},{24,56},{32,64},{40,72},{48,80},{56,88},{64,... | collective-permute-start | bytes 1572872 | tf_op jit(solution)/shard_map/ppermute | solution.py:362
  45.8 1.9 %collective-permute-start.1 = (bf16[2048,128]{1,0:T(8,128)(2,1)S(1)}, bf16[2048,128]{1,0:T(8,128)(2,1)S(1)}, u32[]{:S(2)}, u32[]{:S(2)}) collective-permute-start(bf16[2048,128]{1,0:T(8,128)(2,1)S(1)} %all_gather.3.far), channel_id=1, source_target_pairs={{0,8},{8,0},{16,24},{24,16},{32,40},{40,32},{48,56},{56,48},{64,72... | collective-permute-start | bytes 1572872 | tf_op jit(solution)/shard_map/ppermute | solution.py:366
  47.7 4.0 %collective-permute-start.5 = (bf16[2048,128]{1,0:T(8,128)(2,1)S(1)}, bf16[2048,128]{1,0:T(8,128)(2,1)S(1)}, u32[]{:S(2)}, u32[]{:S(2)}) collective-permute-start(bf16[2048,128]{1,0:T(8,128)(2,1)S(1)} %all_gather.3.far), channel_id=1, source_target_pairs={{0,64},{8,456},{16,80},{24,472},{32,96},{40,488},{48,112},{56,504}... | collective-permute-start | bytes 1572872 | tf_op jit(solution)/shard_map/ppermute | solution.py:364
  51.7 1.8 %collective-permute-done.3.high = bf16[2048,128]{1,0:T(8,128)(2,1)S(1)} collective-permute-done((bf16[2048,128]{1,0:T(8,128)(2,1)S(1)}, bf16[2048,128]{1,0:T(8,128)(2,1)S(1)}, u32[]{:S(2)}, u32[]{:S(2)}) %collective-permute-start.3) | collective-permute-done | bytes 524320 | tf_op jit(solution)/shard_map/ppermute | solution.py:363
  53.5 7.0 %collective-permute-done.2.low = bf16[2048,128]{1,0:T(8,128)(2,1)S(1)} collective-permute-done((bf16[2048,128]{1,0:T(8,128)(2,1)S(1)}, bf16[2048,128]{1,0:T(8,128)(2,1)S(1)}, u32[]{:S(2)}, u32[]{:S(2)}) %collective-permute-start.2) | collective-permute-done | bytes 524320 | tf_op jit(solution)/shard_map/ppermute | solution.py:362
  60.6 3.2 %shard_map.74 = (f32[2,768,128]{2,1,0:T(8,128)S(1)}, f32[2,768,128]{2,1,0:T(8,128)S(1)}, f32[2,768,128]{2,1,0:T(8,128)S(1)}, f32[8,128]{1,0:T(8,128)S(1)}) custom-call(s32[1]{0:T(128)} %bitcast.place, bf16[2,768,128]{2,1,0:T(8,128)(2,1)S(1)} %copy-done.1, bf16[2,768,128]{2,1,0:T(8,128)(2,1)S(1)} %collective-permute-done.q_peer, ...), custom_call_target="tpu_custom_call" | custom-call | flops 905969664 | bytes 4001796 | tf_op jit(solution)/shard_map/pallas_call | solution.py:320
  63.8 8.2 %shard_map.75 = (f32[2,768,128]{2,1,0:T(8,128)S(1)}, f32[2,768,128]{2,1,0:T(8,128)S(1)}, f32[2,768,128]{2,1,0:T(8,128)S(1)}, f32[8,128]{1,0:T(8,128)S(1)}, bf16[4096,128]{1,0:T(8,128)(2,1)S(1)}) custom-call(s32[1]{0:T(128)} %bitcast.place, bf16[2,768,128]{2,1,0:T(8,128)(2,1)S(1)} %copy-done.1, bf16[2,768,128]{2,1,0:T(8,128)(2,1)S(1)} %collective-permute-done.q_peer, ...), custom_call_target="tpu_custom_call" | custom-call | flops 2415919104 | bytes 8134660 | tf_op jit(solution)/shard_map/pallas_call | solution.py:320
  71.9 1.9 %collective-permute-start.4 = (bf16[4096,128]{1,0:T(8,128)(2,1)S(1)}, bf16[4096,128]{1,0:T(8,128)(2,1)S(1)}, u32[]{:S(2)}, u32[]{:S(2)}) collective-permute-start(bf16[4096,128]{1,0:T(8,128)(2,1)S(1)} %get-tuple-element.51), channel_id=1, source_target_pairs={{0,8},{8,0},{16,24},{24,16},{32,40},{40,32},{48,56},{56,48},{64,72... | collective-permute-start | bytes 3145736 | tf_op jit(solution)/shard_map/ppermute | solution.py:385
  73.9 2.4 %collective-permute-start.6 = (bf16[2048,128]{1,0:T(8,128)(2,1)S(1)}, bf16[2048,128]{1,0:T(8,128)(2,1)S(1)}, u32[]{:S(2)}, u32[]{:S(2)}) collective-permute-start(bf16[2048,128]{1,0:T(8,128)(2,1)S(1)} %collective-permute-done.5.near), channel_id=1, source_target_pairs={{0,8},{8,0},{16,24},{24,16},{32,40},{40,32},{48,56},{56,48},{64,72... | collective-permute-start | bytes 1572872 | tf_op jit(solution)/shard_map/ppermute | solution.py:387
  76.3 1.5 %shard_map.77 = (f32[1,768,128]{2,1,0:T(8,128)S(1)}, f32[1,768,128]{2,1,0:T(8,128)S(1)}, f32[1,768,128]{2,1,0:T(8,128)S(1)}) custom-call(s32[1]{0:T(128)} %bitcast.place, bf16[2,768,128]{2,1,0:T(8,128)(2,1)S(1)} %collective-permute-done.q_peer, bf16[2048,128]{1,0:T(8,128)(2,1)S(1)} %collective-permute-done.5.near, ...), custom_call_target="tpu_custom_call" | custom-call | flops 402653184 | bytes 4456452 | tf_op jit(solution)/shard_map/pallas_call | solution.py:320
  77.8 0.1 collective-permute-done.6.three
  77.8 4.2 %shard_map.78 = bf16[816,128]{1,0:T(8,128)(2,1)S(1)} custom-call(s32[1]{0:T(128)} %bitcast.place, bf16[2,768,128]{2,1,0:T(8,128)(2,1)S(1)} %collective-permute-done.q_peer, bf16[4096,128]{1,0:T(8,128)(2,1)S(1)} %collective-permute-done.4.two, bf16[2048,128]{1,0:T(8,128)(2,1)S(1)} %collective-permute-done.6.three, ...), custom_call_target="tpu_custom_call" | custom-call | flops 1207959552 | bytes 3354628 | tf_op jit(solution)/shard_map/pallas_call | solution.py:320
  82.0 5.7 %collective-permute-start.7 = (bf16[816,128]{1,0:T(8,128)(2,1)S(1)}, bf16[816,128]{1,0:T(8,128)(2,1)S(1)}, u32[]{:S(2)}, u32[]{:S(2)}) collective-permute-start(bf16[816,128]{1,0:T(8,128)(2,1)S(1)} %shard_map.78), channel_id=1, source_target_pairs={{0,16},{8,24},{16,0},{24,8},{32,48},{40,56},{48,32},{56,40},{64,80... | collective-permute-start | bytes 626696 | tf_op jit(solution)/shard_map/ppermute | solution.py:393
  87.7 5.1 %shard_map.76 = (f32[1,768,128]{2,1,0:T(8,128)S(1)}, f32[1,768,128]{2,1,0:T(8,128)S(1)}, f32[1,768,128]{2,1,0:T(8,128)S(1)}) custom-call(s32[1]{0:T(128)} %bitcast.place, bf16[2,768,128]{2,1,0:T(8,128)(2,1)S(1)} %copy-done.1, bf16[4096,128]{1,0:T(8,128)(2,1)S(1)} %collective-permute-done.4.two, bf16[2048,128]{1,0:T(8,128)(2,1)S(1)} %collective-permute-done.6.three, ...), custom_call_target="tpu_custom_call" | custom-call | flops 1610612736 | bytes 6033412 | tf_op jit(solution)/shard_map/pallas_call | solution.py:320
  92.9 0.5 collective-permute-done.7.part
  93.4 1.0 shard_map.79
  94.4 28.3 %all_to_all.10.attended = bf16[8,256,384]{2,1,0:T(8,128)(2,1)S(1)} all-to-all(bf16[8,256,384]{2,1,0:T(8,128)(2,1)S(1)} %shard_map.79), channel_id=1, replica_groups=mesh['ctx'=64,'tp'=8] {'tp'}, dimensions={0} | all-to-all | bytes 3145728 | tf_op jit(solution)/shard_map/all_to_all | solution.py:403
  122.7 4.2 %shard_map.80 = bf16[256,640]{1,0:T(8,128)(2,1)} custom-call(bf16[8,256,384]{2,1,0:T(8,128)(2,1)S(1)} %all_to_all.10.attended, bf16[8,384,640]{2,1,0:T(8,128)(2,1)} %all-to-all-done.weight), custom_call_target="tpu_custom_call" | custom-call | flops 1006632960 | bytes 5832704 | tf_op jit(solution)/shard_map/pallas_call | solution.py:320
  (10 shorter events, 0.0 us)
Async XLA Ops:
  5.4 29.0 %collective-permute-start = (bf16[2,768,128]{2,1,0:T(8,128)(2,1)}, bf16[2,768,128]{2,1,0:T(8,128)(2,1)S(1)}, u32[]{:S(2)}, u32[]{:S(2)}) collective-permute-start(bf16[2,768,128]{2,1,0:T(8,128)(2,1)} %get-tuple-element.36.q_own), channel_id=1, source_target_pairs={{0,16},{8,24},{16,0},{24,8},{32,48},{40,56},{48,32},{56,40},{64,80... | collective-permute-start | bytes 1179656 | tf_op jit(solution)/shard_map/ppermute | solution.py:357
  34.4 26.2 %copy-start = (bf16[512,128]{1,0:T(8,128)(2,1)S(1)}, bf16[512,128]{1,0:T(8,128)(2,1)}, u32[]{:S(2)}) copy-start(bf16[512,128]{1,0:T(8,128)(2,1)} %get-tuple-element.42.kv) | copy-start | bytes 393220
  34.4 26.2 %copy-start.1 = (bf16[2,768,128]{2,1,0:T(8,128)(2,1)S(1)}, bf16[2,768,128]{2,1,0:T(8,128)(2,1)}, u32[]{:S(2)}) copy-start(bf16[2,768,128]{2,1,0:T(8,128)(2,1)} %get-tuple-element.36.q_own) | copy-start | bytes 1179652
  34.4 26.1 %copy-start.2 = (bf16[768,128]{1,0:T(8,128)(2,1)S(1)}, bf16[768,128]{1,0:T(8,128)(2,1)}, u32[]{:S(2)}) copy-start(bf16[768,128]{1,0:T(8,128)(2,1)} %get-tuple-element.41.q_intra) | copy-start | bytes 589828
  34.4 60.0 %all-to-all-start = ((bf16[8,384,640]{2,1,0:T(8,128)(2,1)}), bf16[8,384,640]{2,1,0:T(8,128)(2,1)}, u32[]{:S(2)}, u32[]{:S(2)}) async-start(bf16[8,384,640]{2,1,0:T(8,128)(2,1)} %get-tuple-element.64), calls=%async_computation | async-start | bytes 7864320 | tf_op jit(solution)/shard_map/all_to_all | solution.py:360
  39.1 14.4 %collective-permute-start.3 = (bf16[2048,128]{1,0:T(8,128)(2,1)S(1)}, bf16[2048,128]{1,0:T(8,128)(2,1)S(1)}, u32[]{:S(2)}, u32[]{:S(2)}) collective-permute-start(bf16[2048,128]{1,0:T(8,128)(2,1)S(1)} %all_gather.3.far), channel_id=1, source_target_pairs={{0,480},{8,488},{16,496},{24,504},{32,0},{40,8},{48,16},{56,24},{6... | collective-permute-start | bytes 1572872 | tf_op jit(solution)/shard_map/ppermute | solution.py:363
  43.9 16.7 %collective-permute-start.2 = (bf16[2048,128]{1,0:T(8,128)(2,1)S(1)}, bf16[2048,128]{1,0:T(8,128)(2,1)S(1)}, u32[]{:S(2)}, u32[]{:S(2)}) collective-permute-start(bf16[2048,128]{1,0:T(8,128)(2,1)S(1)} %all_gather.3.far), channel_id=1, source_target_pairs={{0,32},{8,40},{16,48},{24,56},{32,64},{40,72},{48,80},{56,88},{64,... | collective-permute-start | bytes 1572872 | tf_op jit(solution)/shard_map/ppermute | solution.py:362
  45.8 18.0 %collective-permute-start.1 = (bf16[2048,128]{1,0:T(8,128)(2,1)S(1)}, bf16[2048,128]{1,0:T(8,128)(2,1)S(1)}, u32[]{:S(2)}, u32[]{:S(2)}) collective-permute-start(bf16[2048,128]{1,0:T(8,128)(2,1)S(1)} %all_gather.3.far), channel_id=1, source_target_pairs={{0,8},{8,0},{16,24},{24,16},{32,40},{40,32},{48,56},{56,48},{64,72... | collective-permute-start | bytes 1572872 | tf_op jit(solution)/shard_map/ppermute | solution.py:366
  47.7 26.2 %collective-permute-start.5 = (bf16[2048,128]{1,0:T(8,128)(2,1)S(1)}, bf16[2048,128]{1,0:T(8,128)(2,1)S(1)}, u32[]{:S(2)}, u32[]{:S(2)}) collective-permute-start(bf16[2048,128]{1,0:T(8,128)(2,1)S(1)} %all_gather.3.far), channel_id=1, source_target_pairs={{0,64},{8,456},{16,80},{24,472},{32,96},{40,488},{48,112},{56,504}... | collective-permute-start | bytes 1572872 | tf_op jit(solution)/shard_map/ppermute | solution.py:364
  71.9 5.9 %collective-permute-start.4 = (bf16[4096,128]{1,0:T(8,128)(2,1)S(1)}, bf16[4096,128]{1,0:T(8,128)(2,1)S(1)}, u32[]{:S(2)}, u32[]{:S(2)}) collective-permute-start(bf16[4096,128]{1,0:T(8,128)(2,1)S(1)} %get-tuple-element.51), channel_id=1, source_target_pairs={{0,8},{8,0},{16,24},{24,16},{32,40},{40,32},{48,56},{56,48},{64,72... | collective-permute-start | bytes 3145736 | tf_op jit(solution)/shard_map/ppermute | solution.py:385
  73.9 3.9 %collective-permute-start.6 = (bf16[2048,128]{1,0:T(8,128)(2,1)S(1)}, bf16[2048,128]{1,0:T(8,128)(2,1)S(1)}, u32[]{:S(2)}, u32[]{:S(2)}) collective-permute-start(bf16[2048,128]{1,0:T(8,128)(2,1)S(1)} %collective-permute-done.5.near), channel_id=1, source_target_pairs={{0,8},{8,0},{16,24},{24,16},{32,40},{40,32},{48,56},{56,48},{64,72... | collective-permute-start | bytes 1572872 | tf_op jit(solution)/shard_map/ppermute | solution.py:387
  82.0 11.4 %collective-permute-start.7 = (bf16[816,128]{1,0:T(8,128)(2,1)S(1)}, bf16[816,128]{1,0:T(8,128)(2,1)S(1)}, u32[]{:S(2)}, u32[]{:S(2)}) collective-permute-start(bf16[816,128]{1,0:T(8,128)(2,1)S(1)} %shard_map.78), channel_id=1, source_target_pairs={{0,16},{8,24},{16,0},{24,8},{32,48},{40,56},{48,32},{56,40},{64,80... | collective-permute-start | bytes 626696 | tf_op jit(solution)/shard_map/ppermute | solution.py:393
